TPU v7x, 32 devices: a whole 2x2x4 slice. The times are simulated.
32 devices in a mesh: section: 4 (over x, core), row: 8 (over z, y).
Axes of the slice: x: 2, y: 2, z: 4, core: 2. Of those that a mesh axis runs over, the one named last changes fastest.
Arguments:
- layer_input: bfloat16 [4, 1024, 4096], P('section', 'row'), may hold values from -6 to 6
- cotangent: bfloat16 [4, 1024, 4096], P('section', 'row'), may hold values from -6 to 6
- route_weight: float32 [4, 1024, 2], P('section', 'row'), may hold values from 0.1 to 0.9
- chosen: int32 [4, 1024, 2], P('section', 'row'), may hold values from 0 to 7, all different within a row
- hot_expert: int32 [4], P('section'), may hold values from 0 to 7
- store_in: bfloat16 [4, 2, 4096, 7168], P('section', None, None, 'row'), may hold values from -0.09375 to 0.09375
- store_out: bfloat16 [4, 7168, 4096], P('section', 'row'), may hold values from -0.0625 to 0.0625
Outputs:
- back_cot: bfloat16 [4, 1024, 4096], P('section', 'row')
- route_grad: float32 [4, 1024, 2], P('section', 'row')
Inputs may be any that keep to these rules, and one draw needn't show every extreme that they name: `chosen`: each token names 2 different experts.
All inputs are finite; a program needn't handle non-finite values.
Results may differ from a plain program's by a relative error of at most 0.0034.
Values may be sent and summed in bfloat16 or wider, within the bound.
A program may use at most 64 MiB of HBM per device.

v0:
```python
import jax
import jax.numpy as jnp
from jax import lax
from jax.sharding import PartitionSpec as P

CAP = 2


def shifted(value, axis, by):
    size = lax.axis_size(axis)
    pairs = [(i, i + by) for i in range(size) if 0 <= i + by < size]
    return lax.ppermute(value, axis, pairs)


def token_select(block_c, hot, slot_count):
    count_tok, top_count = block_c.shape
    hit = (block_c == hot).astype(jnp.int32).reshape(-1)
    order = jnp.cumsum(hit) - hit
    held = hit * (order < slot_count).astype(jnp.int32)
    slots = (order[None, :] == jnp.arange(slot_count, dtype=jnp.int32)[:, None]).astype(
        jnp.int32
    ) * held[None, :]
    tsel = jnp.sum(slots.reshape(slot_count, count_tok, top_count), axis=2)
    return (tsel, held.reshape(count_tok, top_count))


def on_device(layer_input, cotangent, route_weight, chosen, hot_expert, store_in, store_out):
    tokens_here = layer_input[0]
    cot_here = cotangent[0]
    weights_here = route_weight[0]
    width = tokens_here.shape[1]
    num_row = lax.axis_size("row")
    tsel, held = token_select(chosen[0], hot_expert[0], CAP)
    pick = tsel.astype(jnp.bfloat16)
    rows_x = jnp.dot(pick, tokens_here, preferred_element_type=jnp.float32).astype(jnp.bfloat16)
    rows_g = jnp.dot(pick, cot_here, preferred_element_type=jnp.float32).astype(jnp.bfloat16)
    all_x, all_g = (
        lax.all_gather(rows_x, "row", axis=0, tiled=True),
        lax.all_gather(rows_g, "row", axis=0, tiled=True),
    )
    w_gate = store_in[0, 0]
    w_up = store_in[0, 1]
    w_out = store_out[0]
    gate = jnp.dot(all_x, w_gate, preferred_element_type=jnp.float32)
    upper = jnp.dot(all_x, w_up, preferred_element_type=jnp.float32)
    sig = jax.nn.sigmoid(gate)
    hidden = (gate * sig * upper).astype(jnp.bfloat16)
    out_part = jnp.dot(hidden, w_out, preferred_element_type=jnp.float32)
    contract = (((1,), (1,)), ((), ()))
    d_hidden = lax.dot_general(all_g, w_out, contract, preferred_element_type=jnp.float32)
    d_gate = (d_hidden * upper * sig * (1.0 + gate * (1.0 - sig))).astype(jnp.bfloat16)
    d_up = (d_hidden * gate * sig).astype(jnp.bfloat16)
    back_part = lax.dot_general(
        d_gate, w_gate, contract, preferred_element_type=jnp.float32
    ) + lax.dot_general(d_up, w_up, contract, preferred_element_type=jnp.float32)
    score_part = jnp.sum(all_g.astype(jnp.float32) * out_part, axis=1)
    got_back, got_score = (
        lax.all_to_all(
            back_part.reshape(num_row, CAP, width), "row", split_axis=0, concat_axis=0, tiled=True
        ),
        lax.all_to_all(
            score_part.reshape(num_row, CAP), "row", split_axis=0, concat_axis=0, tiled=True
        ),
    )
    back_sum = jnp.sum(got_back, axis=0)
    slot_score = jnp.sum(got_score, axis=0)
    back_rows = back_sum.astype(jnp.bfloat16)
    back_tok = jnp.dot(pick.T, back_rows, preferred_element_type=jnp.float32)
    score_tok = jnp.sum(tsel.astype(jnp.float32).T * slot_score[None, :], axis=1)
    weight_tok = jnp.sum(held.astype(jnp.float32) * weights_here, axis=1)
    cot_float = cot_here.astype(jnp.float32)
    moved = (cot_float + weight_tok[:, None] * back_tok).astype(jnp.bfloat16)
    route_grad = held.astype(jnp.float32) * score_tok[:, None]
    back_cot = shifted(moved, "section", -1)
    return (back_cot[None], route_grad[None])


def solution(mesh):
    in_specs = (
        P("section", "row", None),
        P("section", "row", None),
        P("section", "row", None),
        P("section", "row", None),
        P("section"),
        P("section", None, None, "row"),
        P("section", "row", None),
    )
    out_specs = (P("section", "row", None), P("section", "row", None))
    return jax.shard_map(
        on_device, mesh=mesh, in_specs=in_specs, out_specs=out_specs, check_vma=False
    )
```

profile of v0, /device:TPU:1, one launch (start us, length us, event | category | flops | bytes accessed | tf_op | source)
XLA Modules:
  0.0 122.5 jit_solution(7781455420537622435)
XLA Ops:
  0.6 0.0 copy-start
  1.4 0.7 compare_convert_fusion
  2.1 0.1 copy.29
  2.2 0.1 reshape.142
  2.3 0.3 reduce-window.9
  2.6 0.1 slice.13
  2.7 0.1 reshape.137
  2.9 0.1 slice_reduce_fusion
  3.0 0.1 broadcast.83
  3.1 0.1 reshape.139
  3.2 0.1 copy.30
  3.2 0.7 fusion.38
  4.0 0.0 copy-done
  4.0 0.3 fusion.25
  4.2 25.6 %all-gather.1 = bf16[8,2,4096]{2,1,0:T(2,128)(2,1)S(1)} all-gather(bf16[1,2,4096]{2,1,0:T(2,128)(2,1)S(1)} %fusion.25), channel_id=1, replica_groups=mesh['section'=4,'row'=8] {'row'}, dimensions={0}, use_global_device_ids=true | all-gather | bytes 147456 | tf_op jit(solution)/shard_map/all_gather | solution.py:38
  29.9 0.1 reshape.147
  29.9 0.0 copy-start.1
  29.9 4.2 %fusion.2 = f32[16,896]{1,0:T(8,128)S(1)} fusion(bf16[16,4096]{1,0:T(8,128)(2,1)S(1)} %reshape.147, bf16[1,2,4096,896]{3,2,1,0:T(8,128)(2,1)} %param.12), kind=kOutput, calls=%fused_computation.2 | convolution fusion | flops 117440512 | bytes 7528448 | tf_op jit(solution)/shard_map/dot_general | solution.py:44
  34.2 4.2 %fusion.6 = f32[16,896]{1,0:T(8,128)S(1)} fusion(bf16[16,4096]{1,0:T(8,128)(2,1)S(1)} %reshape.147, bf16[1,2,4096,896]{3,2,1,0:T(8,128)(2,1)} %param.12), kind=kOutput, calls=%fused_computation.6 | convolution fusion | flops 117440512 | bytes 7528448 | tf_op jit(solution)/shard_map/dot_general | solution.py:45
  38.3 0.0 copy-done.1
  38.3 0.3 fusion.24
  38.6 24.4 %all-gather = bf16[8,2,4096]{2,1,0:T(2,128)(2,1)S(1)} all-gather(bf16[1,2,4096]{2,1,0:T(2,128)(2,1)S(1)} %fusion.24), channel_id=1, replica_groups=mesh['section'=4,'row'=8] {'row'}, dimensions={0}, use_global_device_ids=true | all-gather | bytes 147456 | tf_op jit(solution)/shard_map/all_gather | solution.py:39
  63.0 0.1 reshape.145
  63.0 5.1 %fusion.10 = f32[16,896]{1,0:T(8,128)S(1)} fusion(bf16[16,4096]{1,0:T(8,128)(2,1)S(1)} %reshape.145, bf16[1,896,4096]{2,1,0:T(8,128)(2,1)} %param.13), kind=kOutput, calls=%fused_computation.10 | convolution fusion | flops 117440512 | bytes 7528448 | tf_op jit(solution)/shard_map/dot_general | solution.py:50
  68.1 5.1 %fusion = f32[16,4096]{1,0:T(8,128)S(1)} fusion(bf16[1,2,4096,896]{3,2,1,0:T(8,128)(2,1)} %param.12, f32[16,896]{1,0:T(8,128)S(1)} %fusion.2, f32[16,896]{1,0:T(8,128)S(1)} %fusion.10, f32[16,896]{1,0:T(8,128)S(1)} %fusion.6), kind=kOutput, calls=%fused_computation | convolution fusion | flops 117583872 | bytes 7774208 | tf_op jit(solution)/shard_map/dot_general | solution.py:53
  73.2 5.1 %fusion.18 = f32[16,4096]{1,0:T(8,128)S(1)} fusion(f32[16,4096]{1,0:T(8,128)S(1)} %fusion, bf16[1,2,4096,896]{3,2,1,0:T(8,128)(2,1)} %param.12, f32[16,896]{1,0:T(8,128)S(1)} %fusion.10, f32[16,896]{1,0:T(8,128)S(1)} %fusion.2), kind=kOutput, calls=%fused_computation.19 | convolution fusion | flops 117592064 | bytes 7979008 | tf_op jit(solution)/shard_map/dot_general | solution.py:55
  78.3 0.0 copy-start.2
  78.3 0.2 reshape.140
  78.5 11.6 %all_to_all.14 = f32[8,2,4096]{2,1,0:T(2,128)S(1)} all-to-all(f32[8,2,4096]{2,1,0:T(2,128)S(1)} %reshape.140), channel_id=1, replica_groups=mesh['section'=4,'row'=8] {'row'}, dimensions={0} | all-to-all | bytes 524288 | tf_op jit(solution)/shard_map/all_to_all | solution.py:58
  90.1 0.1 reduce_sum.56
  90.2 0.5 fusion.17
  90.7 16.7 %collective-permute-start = (bf16[128,4096]{1,0:T(8,128)(2,1)S(1)}, bf16[128,4096]{1,0:T(8,128)(2,1)S(1)}, u32[]{:S(2)}, u32[]{:S(2)}) collective-permute-start(bf16[128,4096]{1,0:T(8,128)(2,1)S(1)} %fusion.17), channel_id=1, source_target_pairs={{8,0},{16,8},{24,16},{9,1},{17,9},{25,17},{10,2},{18,10},{26,18},{... | collective-permute-start | bytes 3145736 | tf_op jit(solution)/shard_map/ppermute | solution.py:12
  107.4 4.3 %fusion.26 = f32[16]{0:T(128)S(1)} fusion(bf16[1,896,4096]{2,1,0:T(8,128)(2,1)} %param.13, bf16[16,4096]{1,0:T(8,128)(2,1)S(1)} %reshape.145, f32[16,896]{1,0:T(8,128)S(1)} %fusion.6, f32[16,896]{1,0:T(8,128)S(1)} %fusion.2), kind=kOutput, calls=%fused_computation.25 | convolution fusion | flops 117723120 | bytes 7585856 | tf_op jit(solution)/shard_map/dot_general | solution.py:48
  111.7 0.7 all_to_all.10
  112.3 3.3 %all-to-all-start.1 = ((f32[8,1,2]{2,1,0:T(1,128)}), f32[8,1,2]{2,1,0:T(1,128)S(1)}, u32[]{:S(2)}, u32[]{:S(2)}) async-start(f32[8,1,2]{2,1,0:T(1,128)} %bitcast.11), calls=%async_computation.1 | async-start | bytes 8192 | tf_op jit(solution)/shard_map/all_to_all | solution.py:61
  115.7 0.1 reshape.141
  115.8 0.1 copy.31
  115.9 5.0 %all-to-all-done.1 = f32[8,1,2]{2,1,0:T(1,128)S(1)} async-done(((f32[8,1,2]{2,1,0:T(1,128)}), f32[8,1,2]{2,1,0:T(1,128)S(1)}, u32[]{:S(2)}, u32[]{:S(2)}) %all-to-all-start.1) | async-done | bytes 96 | tf_op jit(solution)/shard_map/all_to_all | solution.py:61
  120.9 0.1 multiply_reduce_fusion
  120.9 0.0 copy-done.2
  121.0 0.6 fusion.37
  121.5 0.0 collective-permute-done
  121.5 1.0 copy.35
  (3 shorter events, 0.1 us)
Async XLA Ops:
  0.6 3.4 %copy-start = (bf16[1,128,4096]{2,1,0:T(8,128)(2,1)S(1)}, bf16[1,128,4096]{2,1,0:T(8,128)(2,1)}, u32[]{:S(2)}) copy-start(bf16[1,128,4096]{2,1,0:T(8,128)(2,1)} %param.7) | copy-start | bytes 3145732
  29.9 8.4 %copy-start.1 = (bf16[1,128,4096]{2,1,0:T(8,128)(2,1)S(1)}, bf16[1,128,4096]{2,1,0:T(8,128)(2,1)}, u32[]{:S(2)}) copy-start(bf16[1,128,4096]{2,1,0:T(8,128)(2,1)} %param.8) | copy-start | bytes 3145732
  78.3 42.6 %copy-start.2 = (s32[1,128,2]{1,2,0:T(2,128)S(1)}, s32[1,128,2]{1,2,0:T(2,128)}, u32[]{:S(2)}) copy-start(s32[1,128,2]{1,2,0:T(2,128)} %param.10) | copy-start | bytes 3076
  90.7 30.8 %collective-permute-start = (bf16[128,4096]{1,0:T(8,128)(2,1)S(1)}, bf16[128,4096]{1,0:T(8,128)(2,1)S(1)}, u32[]{:S(2)}, u32[]{:S(2)}) collective-permute-start(bf16[128,4096]{1,0:T(8,128)(2,1)S(1)} %fusion.17), channel_id=1, source_target_pairs={{8,0},{16,8},{24,16},{9,1},{17,9},{25,17},{10,2},{18,10},{26,18},{... | collective-permute-start | bytes 3145736 | tf_op jit(solution)/shard_map/ppermute | solution.py:12
  112.3 8.5 %all-to-all-start.1 = ((f32[8,1,2]{2,1,0:T(1,128)}), f32[8,1,2]{2,1,0:T(1,128)S(1)}, u32[]{:S(2)}, u32[]{:S(2)}) async-start(f32[8,1,2]{2,1,0:T(1,128)} %bitcast.11), calls=%async_computation.1 | async-start | bytes 8192 | tf_op jit(solution)/shard_map/all_to_all | solution.py:61
where the time goes:
time: 123 us; the launch traced here: 122 us
  blocking collectives  61.6 us (50%)
  matrix products  28.9 us (23%)
  starting transfers between devices  20 us (16%)
  waiting for transfers between devices  4.98 us (4%)
  local copies, waits for them, and re-layouts  2.94 us (2%)
  other arithmetic  2.56 us (2%)
  between operations  1.47 us (1%)
    all_gather x1, blocking collectives, on_device(): lax.all_gather(rows_x, 'row', axis=0, tiled=True)  25.6 us
    all_gather x1, blocking collectives, on_device(): lax.all_gather(rows_g, 'row', axis=0, tiled=True)  24.4 us
    ppermute x1, starting transfers between devices, shifted(): return lax.ppermute(value, axis, pairs)  16.7 us
    all_to_all x1, blocking collectives, on_device(): lax.all_to_all(back_part.reshape(num_row, CAP, width), 'row', split_axis=...  11.6 us
    dot_general x1, matrix products, on_device(): lax.dot_general(d_up, w_up, contract, preferred_element_type=jnp.float32)  5.1 us
    dot_general x1, matrix products, on_device(): lax.dot_general(d_gate, w_gate, contract, preferred_element_type=jnp.floa...  5.09 us
    dot_general x1, matrix products, on_device(): lax.dot_general(all_g, w_out, contract, preferred_element_type=jnp.float32)  5.08 us
    all_to_all x1, waiting for transfers between devices, on_device(): lax.all_to_all(score_part.reshape(num_row, CAP), 'row', split_axis=0, con...  4.97 us
  transfers between devices with their start and end apart: 2, of which 1 were waited for; matrix products, arithmetic and copies ran while one was open for 4% of the time, Pallas kernels for 0%

commit v1 on v0

v1 whole, which is shorter than its diff:
```python
import functools

import jax
import jax.numpy as jnp
from jax import lax
from jax.experimental import pallas as pl
from jax.experimental.pallas import tpu as pltpu
from jax.sharding import PartitionSpec as P

CAP = 2
MESH = pl.DeviceIdType.MESH
F32 = jnp.float32
BF16 = jnp.bfloat16
ROWS = 16
PARTS = ROWS // (2 * CAP)
BANDS = ROWS // CAP
HALVES = 2
LAST = (((1,), (1,)), ((), ()))


def iota(shape, dim):
    return lax.broadcasted_iota(jnp.int32, shape, dim)


def expert_kernel(
    n_row, n_sec, hot_ref, chosen_ref, weight_ref, x_hbm, cot_hbm, win_hbm, wout_hbm,
    shift_out, rows_out, scale_out, grad_out,
    x_v, cot_v, win_v, wout_v, gath, xs, gs, zgate, zup, zdh, dgate, dup, back, pack, land,
    scale_v, scale_land, score_v, score_land, zero_v,
    w_sem, t_sem, gath_send, gath_recv, back_send, back_recv, score_send, score_recv,
    small_send, small_recv, shift_send, shift_recv, zero_sem,
):
    sec = lax.axis_index("section")
    me = lax.axis_index("row")
    tokens, width = x_v.shape
    ff = win_v.shape[2]
    slots = n_row * CAP
    part = width // PARTS
    band = width // (HALVES * BANDS)

    def w_copy(i, c):
        if i < 2:
            return pltpu.make_async_copy(
                win_hbm.at[i, pl.ds(c * part, part)], win_v.at[i, pl.ds(c * part, part)], w_sem.at[i, c]
            )
        return pltpu.make_async_copy(
            wout_hbm.at[:, pl.ds(pl.multiple_of(c * part, part), part)], wout_v.at[c], w_sem.at[i, c]
        )

    x_copy = pltpu.make_async_copy(x_hbm, x_v, t_sem.at[0])
    cot_copy = pltpu.make_async_copy(cot_hbm, cot_v, t_sem.at[1])
    x_copy.start()
    cot_copy.start()
    for c in range(PARTS):
        for i in range(3):
            w_copy(i, c).start()

    has_prev = sec > 0
    has_next = sec < n_sec - 1
    barrier = pltpu.get_barrier_semaphore()

    @pl.loop(1, n_row)
    def _(i):
        pl.semaphore_signal(
            barrier, inc=1, device_id={"section": sec, "row": lax.rem(me + i, n_row)}, device_id_type=MESH
        )

    @pl.when(has_prev)
    def _():
        @pl.loop(0, n_row)
        def _(r):
            pl.semaphore_signal(barrier, inc=1, device_id={"section": sec - 1, "row": r}, device_id_type=MESH)

    @pl.when(has_next)
    def _():
        @pl.loop(0, n_row)
        def _(r):
            pl.semaphore_signal(barrier, inc=1, device_id={"section": sec + 1, "row": r}, device_id_type=MESH)

    hit = (chosen_ref[...] == hot_ref[0]).astype(F32)
    hit_tok = jnp.sum(hit, axis=0, keepdims=True)
    before = (iota((tokens, tokens), 0) < iota((tokens, tokens), 1)).astype(BF16)
    order = jnp.dot(
        jnp.broadcast_to(hit_tok, (ROWS, tokens)).astype(BF16), before, preferred_element_type=F32
    )[0:1]
    picks = [jnp.where(order == float(j), hit_tok, 0.0) for j in range(CAP)]
    held = hit * sum(picks)
    weight_tok = jnp.sum(held * weight_ref[...], axis=0, keepdims=True)
    row8 = iota((8, tokens), 0)
    scale = jnp.zeros((8, tokens), F32)
    for j in range(CAP):
        scale = scale + jnp.where(row8 == j, weight_tok * picks[j], 0.0)
    scale_v[...] = scale

    sides = has_prev.astype(jnp.int32) + has_next.astype(jnp.int32)
    pl.semaphore_wait(barrier, n_row - 1 + n_row * sides)

    prev = {"section": sec - 1, "row": me}
    shift = pltpu.make_async_remote_copy(
        cot_hbm, shift_out, shift_send, shift_recv, device_id=prev, device_id_type=MESH
    )
    small = pltpu.make_async_remote_copy(
        scale_v, scale_land, small_send, small_recv, device_id=prev, device_id_type=MESH
    )
    blank = pltpu.make_async_copy(zero_v, shift_out, zero_sem)

    x_copy.wait()
    cot_copy.wait()
    lead = iota((ROWS, tokens), 0)
    block = jnp.zeros((ROWS, part), F32)
    for c in range(PARTS):
        for side, source in enumerate((x_v, cot_v)):
            one = jnp.zeros((ROWS, tokens), F32)
            for j in range(CAP):
                one = one + jnp.where(lead == c * 2 * CAP + side * CAP + j, picks[j], 0.0)
            block = block + jnp.dot(
                one.astype(BF16), source[:, c * part : (c + 1) * part], preferred_element_type=F32
            )
    gath[pl.ds(me, 1)] = block.astype(BF16)[None]

    def gath_copy(i):
        to = lax.rem(me + i, n_row)
        return pltpu.make_async_remote_copy(
            gath.at[me], gath.at[me], gath_send.at[to], gath_recv.at[me],
            device_id={"section": sec, "row": to}, device_id_type=MESH,
        )

    def gath_wait(i):
        src = lax.rem(me + i, n_row)
        return pltpu.make_async_remote_copy(
            gath.at[src], gath.at[src], gath_send.at[src], gath_recv.at[src],
            device_id={"section": sec, "row": src}, device_id_type=MESH,
        )

    @pl.loop(1, n_row)
    def _(i):
        gath_copy(i).start()

    @pl.when(has_prev)
    def _():
        shift.start()
        small.start()

    @pl.when(jnp.logical_not(has_next))
    def _():
        zero_v[...] = jnp.zeros_like(zero_v)
        blank.start()

    @pl.loop(1, n_row)
    def _(i):
        gath_wait(i).wait_recv()

    everyone = gath[...].reshape(n_row * ROWS, part)
    to_row = iota((2 * slots, n_row * ROWS), 0)
    from_row = iota((2 * slots, n_row * ROWS), 1)
    slot = lax.rem(to_row, slots)
    want = (slot // CAP) * ROWS + (to_row // slots) * CAP + lax.rem(slot, CAP)
    for c in range(PARTS):
        sel = (from_row == want + c * 2 * CAP).astype(BF16)
        both = jnp.dot(sel, everyone, preferred_element_type=F32).astype(BF16)
        xs[c] = both[:slots]
        gs[c] = both[slots:]

    zgate[...] = jnp.zeros_like(zgate)
    zup[...] = jnp.zeros_like(zup)
    zdh[...] = jnp.zeros_like(zdh)

    @pl.loop(0, PARTS)
    def _(c):
        rows = pl.ds(pl.multiple_of(c * part, part), part)
        w_copy(0, c).wait()
        zgate[...] += jnp.dot(xs[c], win_v[0, rows, :], preferred_element_type=F32)
        w_copy(1, c).wait()
        zup[...] += jnp.dot(xs[c], win_v[1, rows, :], preferred_element_type=F32)
        w_copy(2, c).wait()
        zdh[...] += lax.dot_general(wout_v[c], gs[c], LAST, preferred_element_type=F32)

    gate, up, dh = zgate[...], zup[...], zdh[...].T
    sig = jax.nn.sigmoid(gate)
    hidden = (gate * sig * up).astype(BF16)
    dgate[...] = (dh * up * sig * (1.0 + gate * (1.0 - sig))).astype(BF16)
    dup[...] = (dh * gate * sig).astype(BF16)
    score = jnp.sum(hidden.astype(F32) * dh, axis=1, keepdims=True)
    diag = iota((slots, 128), 0) == iota((slots, 128), 1)
    score_row = jnp.sum(jnp.where(diag, score, 0.0), axis=0, keepdims=True)
    score_v[...] = jnp.broadcast_to(score_row, score_v.shape)

    def score_copy(to, slot_of):
        return pltpu.make_async_remote_copy(
            score_v, score_land.at[slot_of], score_send.at[to], score_recv.at[slot_of],
            device_id={"section": sec, "row": to}, device_id_type=MESH,
        )

    @pl.loop(1, n_row)
    def _(i):
        score_copy(lax.rem(me + i, n_row), me).start()

    score_land[pl.ds(me, 1)] = score_v[...][None]

    def back_copy(h, r, slot_of):
        return pltpu.make_async_remote_copy(
            pack.at[h, r], land.at[h, slot_of], back_send.at[h, r], back_recv.at[h, slot_of],
            device_id={"section": sec - 1, "row": r}, device_id_type=MESH,
        )

    @pl.when(has_prev)
    def _():
        per = PARTS // HALVES

        @pl.loop(0, HALVES)
        def _(h):
            for q in range(per):
                rows = pl.ds(pl.multiple_of((h * per + q) * part, part), part)
                total = lax.dot_general(win_v[0, rows, :], dgate[...], LAST, preferred_element_type=F32)
                total = total + lax.dot_general(win_v[1, rows, :], dup[...], LAST, preferred_element_type=F32)
                back[:, q * part : (q + 1) * part] = total.T.astype(BF16)
            stack = jnp.concatenate([back[:, b * band : (b + 1) * band] for b in range(BANDS)], axis=0)
            out_row = iota((n_row * ROWS, BANDS * slots), 0)
            in_row = iota((n_row * ROWS, BANDS * slots), 1)
            inner = lax.rem(out_row, ROWS)
            source = (inner // CAP) * slots + (out_row // ROWS) * CAP + lax.rem(inner, CAP)
            perm = (in_row == source).astype(BF16)
            packed = jnp.dot(perm, stack, preferred_element_type=F32).astype(BF16)
            pack[pl.ds(h, 1)] = packed.reshape(1, n_row, ROWS, band)

            @pl.loop(0, n_row)
            def _(r):
                back_copy(h, r, me).start()

    @pl.loop(1, n_row)
    def _(i):
        score_copy(lax.rem(me + i, n_row), lax.rem(me + i, n_row)).wait_recv()

    sums = jnp.sum(score_land[...], axis=0)
    lane = iota(sums.shape, 1)
    grad_tok = jnp.zeros((1, tokens), F32)
    for j in range(CAP):
        mine = jnp.sum(jnp.where(lane == me * CAP + j, sums, 0.0), axis=1, keepdims=True)[0:1]
        grad_tok = grad_tok + picks[j] * mine
    grad_out[...] = held * grad_tok

    @pl.when(has_next)
    def _():
        @pl.loop(0, HALVES)
        def _(h):
            @pl.loop(0, n_row)
            def _(r):
                back_copy(h, r, r).wait_recv()

            total = jnp.sum(land[pl.ds(h, 1)][0].astype(F32), axis=0)
            rows_out[pl.ds(h, 1)] = total.astype(BF16).astype(F32)[None]

        small.wait_recv()
        shift.wait_recv()
        scale_out[...] = scale_land[...]

    @pl.when(jnp.logical_not(has_next))
    def _():
        rows_out[...] = jnp.zeros_like(rows_out)
        scale_out[...] = jnp.zeros_like(scale_out)
        blank.wait()

    @pl.loop(1, n_row)
    def _(i):
        gath_copy(i).wait_send()
        score_copy(lax.rem(me + i, n_row), me).wait_send()

    @pl.when(has_prev)
    def _():
        shift.wait_send()
        small.wait_send()

        @pl.loop(0, HALVES)
        def _(h):
            @pl.loop(0, n_row)
            def _(r):
                back_copy(h, r, me).wait_send()


def merge_kernel(shift_ref, rows_ref, scale_ref, out_ref):
    tokens = shift_ref.shape[0]
    band = rows_ref.shape[2]
    diag = iota((tokens, tokens), 0) == iota((tokens, tokens), 1)
    cols = [
        jnp.sum(jnp.where(diag, scale_ref[j : j + 1, :], 0.0), axis=1, keepdims=True) for j in range(CAP)
    ]
    for b in range(BANDS):
        at = slice(b * band, (b + 1) * band)
        value = shift_ref[:, at].astype(F32)
        for j in range(CAP):
            value = value + cols[j] * rows_ref[0, b * CAP + j : b * CAP + j + 1, :]
        out_ref[:, at] = value.astype(BF16)


def on_device(n_row, n_sec, layer_input, cotangent, route_weight, chosen, hot_expert, store_in, store_out):
    _, tokens, width = layer_input.shape
    ff = store_out.shape[1]
    top = chosen.shape[2]
    slots = n_row * CAP
    part = width // PARTS
    band = width // (HALVES * BANDS)
    hbm = pl.BlockSpec(memory_space=pl.ANY)
    vmem = pl.BlockSpec(memory_space=pltpu.VMEM)
    dma = pltpu.SemaphoreType.DMA
    shift, rows, scale, grad = pl.pallas_call(
        functools.partial(expert_kernel, n_row, n_sec),
        out_shape=(
            jax.ShapeDtypeStruct((tokens, width), BF16),
            jax.ShapeDtypeStruct((HALVES, ROWS, band), F32),
            jax.ShapeDtypeStruct((8, tokens), F32),
            jax.ShapeDtypeStruct((top, tokens), F32),
        ),
        in_specs=[pl.BlockSpec(memory_space=pltpu.SMEM), vmem, vmem, hbm, hbm, hbm, hbm],
        out_specs=(hbm, vmem, vmem, vmem),
        scratch_shapes=[
            pltpu.VMEM((tokens, width), BF16),
            pltpu.VMEM((tokens, width), BF16),
            pltpu.VMEM((2, width, ff), BF16),
            pltpu.VMEM((PARTS, ff, part), BF16),
            pltpu.VMEM((n_row, ROWS, part), BF16),
            pltpu.VMEM((PARTS, slots, part), BF16),
            pltpu.VMEM((PARTS, slots, part), BF16),
            pltpu.VMEM((slots, ff), F32),
            pltpu.VMEM((slots, ff), F32),
            pltpu.VMEM((ff, slots), F32),
            pltpu.VMEM((slots, ff), BF16),
            pltpu.VMEM((slots, ff), BF16),
            pltpu.VMEM((slots, width // HALVES), BF16),
            pltpu.VMEM((HALVES, n_row, ROWS, band), BF16),
            pltpu.VMEM((HALVES, n_row, ROWS, band), BF16),
            pltpu.VMEM((8, tokens), F32),
            pltpu.VMEM((8, tokens), F32),
            pltpu.VMEM((8, 128), F32),
            pltpu.VMEM((n_row, 8, 128), F32),
            pltpu.VMEM((tokens, width), BF16),
            dma((3, PARTS)),
            dma((2,)),
            dma((n_row,)),
            dma((n_row,)),
            dma((HALVES, n_row)),
            dma((HALVES, n_row)),
            dma((n_row,)),
            dma((n_row,)),
            dma,
            dma,
            dma,
            dma,
            dma,
        ],
        compiler_params=pltpu.CompilerParams(
            collective_id=0, has_side_effects=True, vmem_limit_bytes=60 * 2**20
        ),
        cost_estimate=pl.CostEstimate(
            flops=10 * slots * width * ff, bytes_accessed=6 * width * ff, transcendentals=slots * ff
        ),
        name="expert",
    )(
        hot_expert,
        jnp.transpose(chosen[0]),
        jnp.transpose(route_weight[0]),
        layer_input[0],
        cotangent[0],
        store_in[0],
        store_out[0],
    )
    half = width // HALVES
    moved = pl.pallas_call(
        merge_kernel,
        out_shape=jax.ShapeDtypeStruct((tokens, width), BF16),
        grid=(HALVES,),
        in_specs=[
            pl.BlockSpec((tokens, half), lambda h: (0, h)),
            pl.BlockSpec((1, ROWS, band), lambda h: (h, 0, 0)),
            pl.BlockSpec((8, tokens), lambda h: (0, 0)),
        ],
        out_specs=pl.BlockSpec((tokens, half), lambda h: (0, h)),
        name="merge",
    )(shift, rows, scale)
    return (moved[None], jnp.transpose(grad)[None])


def token_select(block_c, hot, slot_count):
    count_tok, top_count = block_c.shape
    hit = (block_c == hot).astype(jnp.int32).reshape(-1)
    order = jnp.cumsum(hit) - hit
    held = hit * (order < slot_count).astype(jnp.int32)
    slots = (order[None, :] == jnp.arange(slot_count, dtype=jnp.int32)[:, None]).astype(
        jnp.int32
    ) * held[None, :]
    tsel = jnp.sum(slots.reshape(slot_count, count_tok, top_count), axis=2)
    return (tsel, held.reshape(count_tok, top_count))


def on_device_narrow(layer_input, cotangent, route_weight, chosen, hot_expert, store_in, store_out):
    tokens_here = layer_input[0]
    cot_here = cotangent[0]
    width = tokens_here.shape[1]
    num_row = lax.axis_size("row")
    size = lax.axis_size("section")
    tsel, held = token_select(chosen[0], hot_expert[0], CAP)
    pick = tsel.astype(BF16)
    rows = jnp.concatenate(
        [jnp.dot(pick, part, preferred_element_type=F32).astype(BF16) for part in (tokens_here, cot_here)], axis=1
    )
    both = lax.all_gather(rows, "row", axis=0, tiled=True)
    all_x, all_g = both[:, :width], both[:, width:]
    w_gate, w_up, w_out = store_in[0, 0], store_in[0, 1], store_out[0]
    gate = jnp.dot(all_x, w_gate, preferred_element_type=F32)
    upper = jnp.dot(all_x, w_up, preferred_element_type=F32)
    sig = jax.nn.sigmoid(gate)
    hidden = (gate * sig * upper).astype(BF16)
    d_hidden = lax.dot_general(all_g, w_out, LAST, preferred_element_type=F32)
    d_gate = (d_hidden * upper * sig * (1.0 + gate * (1.0 - sig))).astype(BF16)
    d_up = (d_hidden * gate * sig).astype(BF16)
    back_part = lax.dot_general(d_gate, w_gate, LAST, preferred_element_type=F32) + lax.dot_general(
        d_up, w_up, LAST, preferred_element_type=F32
    )
    score_part = jnp.sum(hidden.astype(F32) * d_hidden, axis=1)
    got_back = lax.all_to_all(
        back_part.reshape(num_row, CAP, width), "row", split_axis=0, concat_axis=0, tiled=True
    )
    got_score = lax.all_to_all(
        score_part.reshape(num_row, CAP), "row", split_axis=0, concat_axis=0, tiled=True
    )
    back_rows = jnp.sum(got_back, axis=0).astype(BF16)
    slot_score = jnp.sum(got_score, axis=0)
    back_tok = jnp.dot(pick.T, back_rows, preferred_element_type=F32)
    score_tok = jnp.sum(tsel.astype(F32).T * slot_score[None, :], axis=1)
    weight_tok = jnp.sum(held.astype(F32) * route_weight[0], axis=1)
    moved = (cot_here.astype(F32) + weight_tok[:, None] * back_tok).astype(BF16)
    route_grad = held.astype(F32) * score_tok[:, None]
    back_cot = lax.ppermute(moved, "section", [(i, i - 1) for i in range(1, size)])
    return (back_cot[None], route_grad[None])


def solution(mesh):
    n_row, n_sec = mesh.shape["row"], mesh.shape["section"]

    def body(layer_input, cotangent, route_weight, chosen, hot_expert, store_in, store_out):
        args = (layer_input, cotangent, route_weight, chosen, hot_expert, store_in, store_out)
        if store_out.shape[1] % 128 or n_row * CAP > 128:
            return on_device_narrow(*args)
        return on_device(n_row, n_sec, *args)

    in_specs = (
        P("section", "row", None),
        P("section", "row", None),
        P("section", "row", None),
        P("section", "row", None),
        P("section"),
        P("section", None, None, "row"),
        P("section", "row", None),
    )
    out_specs = (P("section", "row", None), P("section", "row", None))
    return jax.shard_map(body, mesh=mesh, in_specs=in_specs, out_specs=out_specs, check_vma=False)
```

time: 123 us -> 40.4 us (0.33)
  blocking collectives: 61.6 us -> 0 us
  Pallas kernels: 0 us -> 37.8 us
  matrix products: 28.9 us -> 0 us
  starting transfers between devices: 20 us -> 0 us
  waiting for transfers between devices: 4.98 us -> 0 us
  other arithmetic: 2.56 us -> 0 us
  local copies, waits for them, and re-layouts: 2.94 us -> 1.22 us
    all_gather x2 -> x0, blocking collectives: 50 us -> none  [the longest x1 25.6 us: on_device(): lax.all_gather(rows_x, 'row', axis=0, tiled=True)]
    pallas_call x0 -> x2, Pallas kernels: none -> 37.8 us  [the longest x1 35.3 us: on_device(): pl.pallas_call(functools.partial(expert_kernel, n_row, n_sec), out_shape=...]
    dot_general x9 -> x0, matrix products: 28.9 us -> none  [the longest x1 5.1 us: on_device(): lax.dot_general(d_up, w_up, contract, preferred_element_type=jnp.float32)]
    ppermute x1 -> x0, starting transfers between devices: 16.7 us -> none  [shifted(): return lax.ppermute(value, axis, pairs)]
    all_to_all x1 -> x0, blocking collectives: 11.6 us -> none  [on_device(): lax.all_to_all(back_part.reshape(num_row, CAP, width), 'row', split_axis=...]
    all_to_all x1 -> x0, waiting for transfers between devices: 4.97 us -> none  [on_device(): lax.all_to_all(score_part.reshape(num_row, CAP), 'row', split_axis=0, con...]
    all_to_all x1 -> x0, starting transfers between devices: 3.31 us -> none  [on_device(): lax.all_to_all(score_part.reshape(num_row, CAP), 'row', split_axis=0, con...]
  transfers between devices with their start and end apart: 2 -> 0, of which waited for: 1 -> 0; matrix products, arithmetic and copies ran while one was open for 4% -> 0% of each run, Pallas kernels for 0% -> 0%
where the time goes in v1:
time: 40.4 us; the launch traced here: 40.3 us
  Pallas kernels  37.8 us (94%)
  between operations  1.29 us (3%)
  local copies, waits for them, and re-layouts  1.22 us (3%)
    pallas_call x1, Pallas kernels, on_device(): pl.pallas_call(functools.partial(expert_kernel, n_row, n_sec), out_shape=...  35.3 us
    pallas_call x1, Pallas kernels, on_device(): pl.pallas_call(merge_kernel, out_shape=jax.ShapeDtypeStruct((tokens, widt...  2.42 us
    unnamed x1, local copies, waits for them, and re-layouts  1.22 us

profile of v1, /device:TPU:1, one launch (start us, length us, event | category | flops | bytes accessed | tf_op | source)
XLA Modules:
  0.0 40.3 jit_solution(7052343299483661676)
XLA Ops:
  1.3 35.3 %expert.1 = (bf16[128,4096]{1,0:T(8,128)(2,1)}, f32[2,16,256]{2,1,0:T(8,128)}, f32[8,128]{1,0:T(8,128)}, f32[2,128]{1,0:T(2,128)}) custom-call(s32[1]{0:T(128)S(6)} %copy.10.hot_ref, s32[2,128]{1,0:T(2,128)} %bitcast.19, f32[2,128]{1,0:T(2,128)} %bitcast.20, bf16[128,4096]{1,0:T(8,128)(2,1)} %bitcast.16, bf16[128,4096]{1,0:T(8,128)(2,1)} %bitcast.17, ...), custom_call_target="tpu_custom_call" | custom-call | flops 587202560 | bytes 22020096 | tf_op jit(solution)/shard_map/expert/pallas_call | solution.py:305
  36.6 2.4 %merge.1 = bf16[128,4096]{1,0:T(8,128)(2,1)} custom-call(bf16[128,4096]{1,0:T(8,128)(2,1)} %get-tuple-element.6.shift_ref, f32[2,16,256]{2,1,0:T(8,128)} %get-tuple-element.7.rows_ref, f32[8,128]{1,0:T(8,128)} %get-tuple-element.8.scale_ref), custom_call_target="tpu_custom_call" | custom-call | tf_op jit(solution)/shard_map/merge/pallas_call | solution.py:367
  39.0 1.2 %copy.11 = f32[1,128,2]{1,2,0:T(2,128)} copy(f32[1,128,2]{1,2,0:T(2,128)} %bitcast.21) | data formatting | bytes 2048

commit v2 on v1

--- a/solution.py
+++ b/solution.py
@@ -12,9 +12,8 @@
 F32 = jnp.float32
 BF16 = jnp.bfloat16
 ROWS = 16
-PARTS = ROWS // (2 * CAP)
 BANDS = ROWS // CAP
-HALVES = 2
+QUARTERS = 4
 LAST = (((1,), (1,)), ((), ()))
 
 
@@ -25,35 +24,28 @@
 def expert_kernel(
     n_row, n_sec, hot_ref, chosen_ref, weight_ref, x_hbm, cot_hbm, win_hbm, wout_hbm,
     shift_out, rows_out, scale_out, grad_out,
-    x_v, cot_v, win_v, wout_v, gath, xs, gs, zgate, zup, zdh, dgate, dup, back, pack, land,
+    x_v, cot_v, win_v, wout_v, gath, xs, gs, pack, land,
     scale_v, scale_land, score_v, score_land, zero_v,
-    w_sem, t_sem, gath_send, gath_recv, back_send, back_recv, score_send, score_recv,
+    win_sem, wout_sem, t_sem, gath_send, gath_recv, back_send, back_recv, score_send, score_recv,
     small_send, small_recv, shift_send, shift_recv, zero_sem,
 ):
     sec = lax.axis_index("section")
     me = lax.axis_index("row")
     tokens, width = x_v.shape
-    ff = win_v.shape[2]
     slots = n_row * CAP
-    part = width // PARTS
-    band = width // (HALVES * BANDS)
-
-    def w_copy(i, c):
-        if i < 2:
-            return pltpu.make_async_copy(
-                win_hbm.at[i, pl.ds(c * part, part)], win_v.at[i, pl.ds(c * part, part)], w_sem.at[i, c]
-            )
-        return pltpu.make_async_copy(
-            wout_hbm.at[:, pl.ds(pl.multiple_of(c * part, part), part)], wout_v.at[c], w_sem.at[i, c]
-        )
-
+    part = width // BANDS
+    quarter = width // QUARTERS
+    band = quarter // BANDS
+
+    def win_copy(i, c):
+        rows = pl.ds(c * quarter, quarter)
+        return pltpu.make_async_copy(win_hbm.at[i, rows], win_v.at[i, rows], win_sem.at[i, c])
+
+    wout_copy = pltpu.make_async_copy(wout_hbm, wout_v, wout_sem)
     x_copy = pltpu.make_async_copy(x_hbm, x_v, t_sem.at[0])
     cot_copy = pltpu.make_async_copy(cot_hbm, cot_v, t_sem.at[1])
     x_copy.start()
     cot_copy.start()
-    for c in range(PARTS):
-        for i in range(3):
-            w_copy(i, c).start()
 
     has_prev = sec > 0
     has_next = sec < n_sec - 1
@@ -92,8 +84,27 @@
         scale = scale + jnp.where(row8 == j, weight_tok * picks[j], 0.0)
     scale_v[...] = scale
 
-    sides = has_prev.astype(jnp.int32) + has_next.astype(jnp.int32)
-    pl.semaphore_wait(barrier, n_row - 1 + n_row * sides)
+    lead = iota((ROWS, tokens), 0)
+    ones = []
+    for c in range(BANDS):
+        one = jnp.zeros((ROWS, tokens), F32)
+        for j in range(CAP):
+            one = one + jnp.where(lead == c * CAP + j, picks[j], 0.0)
+        ones.append(one.astype(BF16))
+
+    def held_rows(source):
+        block = jnp.zeros((ROWS, part), F32)
+        for c in range(BANDS):
+            block = block + jnp.dot(
+                ones[c], source[:, c * part : (c + 1) * part], preferred_element_type=F32
+            )
+        return block.astype(BF16)
+
+    def gath_copy(k, to, slot_of):
+        return pltpu.make_async_remote_copy(
+            gath.at[k, slot_of], gath.at[k, slot_of], gath_send.at[k, to], gath_recv.at[k, slot_of],
+            device_id={"section": sec, "row": to}, device_id_type=MESH,
+        )
 
     prev = {"section": sec - 1, "row": me}
     shift = pltpu.make_async_remote_copy(
@@ -105,36 +116,26 @@
     blank = pltpu.make_async_copy(zero_v, shift_out, zero_sem)
 
     x_copy.wait()
+    gath[0, pl.ds(me, 1)] = held_rows(x_v)[None]
+
+    sides = has_prev.astype(jnp.int32) + has_next.astype(jnp.int32)
+    pl.semaphore_wait(barrier, n_row - 1 + n_row * sides)
+
+    @pl.loop(1, n_row)
+    def _(i):
+        gath_copy(0, lax.rem(me + i, n_row), me).start()
+
     cot_copy.wait()
-    lead = iota((ROWS, tokens), 0)
-    block = jnp.zeros((ROWS, part), F32)
-    for c in range(PARTS):
-        for side, source in enumerate((x_v, cot_v)):
-            one = jnp.zeros((ROWS, tokens), F32)
-            for j in range(CAP):
-                one = one + jnp.where(lead == c * 2 * CAP + side * CAP + j, picks[j], 0.0)
-            block = block + jnp.dot(
-                one.astype(BF16), source[:, c * part : (c + 1) * part], preferred_element_type=F32
-            )
-    gath[pl.ds(me, 1)] = block.astype(BF16)[None]
-
-    def gath_copy(i):
-        to = lax.rem(me + i, n_row)
-        return pltpu.make_async_remote_copy(
-            gath.at[me], gath.at[me], gath_send.at[to], gath_recv.at[me],
-            device_id={"section": sec, "row": to}, device_id_type=MESH,
-        )
-
-    def gath_wait(i):
-        src = lax.rem(me + i, n_row)
-        return pltpu.make_async_remote_copy(
-            gath.at[src], gath.at[src], gath_send.at[src], gath_recv.at[src],
-            device_id={"section": sec, "row": src}, device_id_type=MESH,
-        )
-
-    @pl.loop(1, n_row)
-    def _(i):
-        gath_copy(i).start()
+    for c in range(QUARTERS):
+        win_copy(0, c).start()
+        win_copy(1, c).start()
+    wout_copy.start()
+
+    gath[1, pl.ds(me, 1)] = held_rows(cot_v)[None]
+
+    @pl.loop(1, n_row)
+    def _(i):
+        gath_copy(1, lax.rem(me + i, n_row), me).start()
 
     @pl.when(has_prev)
     def _():
@@ -146,40 +147,41 @@
         zero_v[...] = jnp.zeros_like(zero_v)
         blank.start()
 
-    @pl.loop(1, n_row)
-    def _(i):
-        gath_wait(i).wait_recv()
-
-    everyone = gath[...].reshape(n_row * ROWS, part)
-    to_row = iota((2 * slots, n_row * ROWS), 0)
-    from_row = iota((2 * slots, n_row * ROWS), 1)
+    to_row = iota((BANDS * slots, n_row * ROWS), 0)
     slot = lax.rem(to_row, slots)
     want = (slot // CAP) * ROWS + (to_row // slots) * CAP + lax.rem(slot, CAP)
-    for c in range(PARTS):
-        sel = (from_row == want + c * 2 * CAP).astype(BF16)
-        both = jnp.dot(sel, everyone, preferred_element_type=F32).astype(BF16)
-        xs[c] = both[:slots]
-        gs[c] = both[slots:]
-
-    zgate[...] = jnp.zeros_like(zgate)
-    zup[...] = jnp.zeros_like(zup)
-    zdh[...] = jnp.zeros_like(zdh)
-
-    @pl.loop(0, PARTS)
-    def _(c):
-        rows = pl.ds(pl.multiple_of(c * part, part), part)
-        w_copy(0, c).wait()
-        zgate[...] += jnp.dot(xs[c], win_v[0, rows, :], preferred_element_type=F32)
-        w_copy(1, c).wait()
-        zup[...] += jnp.dot(xs[c], win_v[1, rows, :], preferred_element_type=F32)
-        w_copy(2, c).wait()
-        zdh[...] += lax.dot_general(wout_v[c], gs[c], LAST, preferred_element_type=F32)
-
-    gate, up, dh = zgate[...], zup[...], zdh[...].T
+    spread = (iota((BANDS * slots, n_row * ROWS), 1) == want).astype(BF16)
+
+    def gathered(k, rows_ref):
+        @pl.loop(1, n_row)
+        def _(i):
+            src = lax.rem(me + i, n_row)
+            gath_copy(k, src, src).wait_recv()
+
+        everyone = gath[k].reshape(n_row * ROWS, part)
+        rows = jnp.dot(spread, everyone, preferred_element_type=F32).astype(BF16)
+        for c in range(BANDS):
+            rows_ref[:, c * part : (c + 1) * part] = rows[c * slots : (c + 1) * slots]
+
+    gathered(0, xs)
+    gate = up = None
+    for c in range(QUARTERS):
+        cols = slice(c * quarter, (c + 1) * quarter)
+        win_copy(0, c).wait()
+        win_copy(1, c).wait()
+        g_part = jnp.dot(xs[:, cols], win_v[0, cols, :], preferred_element_type=F32)
+        u_part = jnp.dot(xs[:, cols], win_v[1, cols, :], preferred_element_type=F32)
+        gate = g_part if gate is None else gate + g_part
+        up = u_part if up is None else up + u_part
+
+    gathered(1, gs)
+    wout_copy.wait()
+    dh = lax.dot_general(wout_v[...], gs[...], LAST, preferred_element_type=F32).T
+
     sig = jax.nn.sigmoid(gate)
     hidden = (gate * sig * up).astype(BF16)
-    dgate[...] = (dh * up * sig * (1.0 + gate * (1.0 - sig))).astype(BF16)
-    dup[...] = (dh * gate * sig).astype(BF16)
+    dgate = (dh * up * sig * (1.0 + gate * (1.0 - sig))).astype(BF16)
+    dup = (dh * gate * sig).astype(BF16)
     score = jnp.sum(hidden.astype(F32) * dh, axis=1, keepdims=True)
     diag = iota((slots, 128), 0) == iota((slots, 128), 1)
     score_row = jnp.sum(jnp.where(diag, score, 0.0), axis=0, keepdims=True)
@@ -197,39 +199,35 @@
 
     score_land[pl.ds(me, 1)] = score_v[...][None]
 
-    def back_copy(h, r, slot_of):
+    def back_copy(q, r, slot_of):
         return pltpu.make_async_remote_copy(
-            pack.at[h, r], land.at[h, slot_of], back_send.at[h, r], back_recv.at[h, slot_of],
+            pack.at[q, r], land.at[q, slot_of], back_send.at[q, r], back_recv.at[q, slot_of],
             device_id={"section": sec - 1, "row": r}, device_id_type=MESH,
         )
 
     @pl.when(has_prev)
     def _():
-        per = PARTS // HALVES
-
-        @pl.loop(0, HALVES)
-        def _(h):
-            for q in range(per):
-                rows = pl.ds(pl.multiple_of((h * per + q) * part, part), part)
-                total = lax.dot_general(win_v[0, rows, :], dgate[...], LAST, preferred_element_type=F32)
-                total = total + lax.dot_general(win_v[1, rows, :], dup[...], LAST, preferred_element_type=F32)
-                back[:, q * part : (q + 1) * part] = total.T.astype(BF16)
+        out_row = iota((n_row * ROWS, BANDS * slots), 0)
+        inner = lax.rem(out_row, ROWS)
+        source = (inner // CAP) * slots + (out_row // ROWS) * CAP + lax.rem(inner, CAP)
+        perm = (iota((n_row * ROWS, BANDS * slots), 1) == source).astype(BF16)
+        for q in range(QUARTERS):
+            rows = slice(q * quarter, (q + 1) * quarter)
+            total = lax.dot_general(win_v[0, rows, :], dgate, LAST, preferred_element_type=F32)
+            total = total + lax.dot_general(win_v[1, rows, :], dup, LAST, preferred_element_type=F32)
+            back = total.T.astype(BF16)
             stack = jnp.concatenate([back[:, b * band : (b + 1) * band] for b in range(BANDS)], axis=0)
-            out_row = iota((n_row * ROWS, BANDS * slots), 0)
-            in_row = iota((n_row * ROWS, BANDS * slots), 1)
-            inner = lax.rem(out_row, ROWS)
-            source = (inner // CAP) * slots + (out_row // ROWS) * CAP + lax.rem(inner, CAP)
-            perm = (in_row == source).astype(BF16)
             packed = jnp.dot(perm, stack, preferred_element_type=F32).astype(BF16)
-            pack[pl.ds(h, 1)] = packed.reshape(1, n_row, ROWS, band)
+            pack[q] = packed.reshape(n_row, ROWS, band)
 
             @pl.loop(0, n_row)
             def _(r):
-                back_copy(h, r, me).start()
-
-    @pl.loop(1, n_row)
-    def _(i):
-        score_copy(lax.rem(me + i, n_row), lax.rem(me + i, n_row)).wait_recv()
+                back_copy(q, r, me).start()
+
+    @pl.loop(1, n_row)
+    def _(i):
+        src = lax.rem(me + i, n_row)
+        score_copy(src, src).wait_recv()
 
     sums = jnp.sum(score_land[...], axis=0)
     lane = iota(sums.shape, 1)
@@ -241,18 +239,15 @@
 
     @pl.when(has_next)
     def _():
-        @pl.loop(0, HALVES)
-        def _(h):
+        small.wait_recv()
+        scale_out[...] = scale_land[...]
+        shift.wait_recv()
+        for q in range(QUARTERS):
             @pl.loop(0, n_row)
             def _(r):
-                back_copy(h, r, r).wait_recv()
-
-            total = jnp.sum(land[pl.ds(h, 1)][0].astype(F32), axis=0)
-            rows_out[pl.ds(h, 1)] = total.astype(BF16).astype(F32)[None]
-
-        small.wait_recv()
-        shift.wait_recv()
-        scale_out[...] = scale_land[...]
+                back_copy(q, r, r).wait_recv()
+
+            rows_out[q] = jnp.sum(land[q].astype(F32), axis=0).astype(BF16).astype(F32)
 
     @pl.when(jnp.logical_not(has_next))
     def _():
@@ -262,28 +257,34 @@
 
     @pl.loop(1, n_row)
     def _(i):
-        gath_copy(i).wait_send()
-        score_copy(lax.rem(me + i, n_row), me).wait_send()
+        to = lax.rem(me + i, n_row)
+        gath_copy(0, to, me).wait_send()
+        gath_copy(1, to, me).wait_send()
+        score_copy(to, me).wait_send()
 
     @pl.when(has_prev)
     def _():
         shift.wait_send()
         small.wait_send()
 
-        @pl.loop(0, HALVES)
-        def _(h):
-            @pl.loop(0, n_row)
-            def _(r):
-                back_copy(h, r, me).wait_send()
-
-
-def merge_kernel(shift_ref, rows_ref, scale_ref, out_ref):
+        @pl.loop(0, n_row)
+        def _(r):
+            for q in range(QUARTERS):
+                back_copy(q, r, me).wait_send()
+
+
+def merge_kernel(shift_ref, rows_ref, scale_ref, grad_ref, out_ref, grad_out, cols):
     tokens = shift_ref.shape[0]
     band = rows_ref.shape[2]
-    diag = iota((tokens, tokens), 0) == iota((tokens, tokens), 1)
-    cols = [
-        jnp.sum(jnp.where(diag, scale_ref[j : j + 1, :], 0.0), axis=1, keepdims=True) for j in range(CAP)
-    ]
+
+    @pl.when(pl.program_id(0) == 0)
+    def _():
+        grad_out[...] = grad_ref[...]
+        diag = iota((tokens, tokens), 0) == iota((tokens, tokens), 1)
+        for j in range(CAP):
+            col = jnp.sum(jnp.where(diag, scale_ref[j : j + 1, :], 0.0), axis=1, keepdims=True)
+            cols[j] = jnp.broadcast_to(col, (tokens, band))
+
     for b in range(BANDS):
         at = slice(b * band, (b + 1) * band)
         value = shift_ref[:, at].astype(F32)
@@ -297,8 +298,9 @@
     ff = store_out.shape[1]
     top = chosen.shape[2]
     slots = n_row * CAP
-    part = width // PARTS
-    band = width // (HALVES * BANDS)
+    part = width // BANDS
+    quarter = width // QUARTERS
+    band = quarter // BANDS
     hbm = pl.BlockSpec(memory_space=pl.ANY)
     vmem = pl.BlockSpec(memory_space=pltpu.VMEM)
     dma = pltpu.SemaphoreType.DMA
@@ -306,7 +308,7 @@
         functools.partial(expert_kernel, n_row, n_sec),
         out_shape=(
             jax.ShapeDtypeStruct((tokens, width), BF16),
-            jax.ShapeDtypeStruct((HALVES, ROWS, band), F32),
+            jax.ShapeDtypeStruct((QUARTERS, ROWS, band), F32),
             jax.ShapeDtypeStruct((8, tokens), F32),
             jax.ShapeDtypeStruct((top, tokens), F32),
         ),
@@ -316,29 +318,24 @@
             pltpu.VMEM((tokens, width), BF16),
             pltpu.VMEM((tokens, width), BF16),
             pltpu.VMEM((2, width, ff), BF16),
-            pltpu.VMEM((PARTS, ff, part), BF16),
-            pltpu.VMEM((n_row, ROWS, part), BF16),
-            pltpu.VMEM((PARTS, slots, part), BF16),
-            pltpu.VMEM((PARTS, slots, part), BF16),
-            pltpu.VMEM((slots, ff), F32),
-            pltpu.VMEM((slots, ff), F32),
-            pltpu.VMEM((ff, slots), F32),
-            pltpu.VMEM((slots, ff), BF16),
-            pltpu.VMEM((slots, ff), BF16),
-            pltpu.VMEM((slots, width // HALVES), BF16),
-            pltpu.VMEM((HALVES, n_row, ROWS, band), BF16),
-            pltpu.VMEM((HALVES, n_row, ROWS, band), BF16),
+            pltpu.VMEM((ff, width), BF16),
+            pltpu.VMEM((2, n_row, ROWS, part), BF16),
+            pltpu.VMEM((slots, width), BF16),
+            pltpu.VMEM((slots, width), BF16),
+            pltpu.VMEM((QUARTERS, n_row, ROWS, band), BF16),
+            pltpu.VMEM((QUARTERS, n_row, ROWS, band), BF16),
             pltpu.VMEM((8, tokens), F32),
             pltpu.VMEM((8, tokens), F32),
             pltpu.VMEM((8, 128), F32),
             pltpu.VMEM((n_row, 8, 128), F32),
             pltpu.VMEM((tokens, width), BF16),
-            dma((3, PARTS)),
+            dma((2, QUARTERS)),
+            dma,
             dma((2,)),
-            dma((n_row,)),
-            dma((n_row,)),
-            dma((HALVES, n_row)),
-            dma((HALVES, n_row)),
+            dma((2, n_row)),
+            dma((2, n_row)),
+            dma((QUARTERS, n_row)),
+            dma((QUARTERS, n_row)),
             dma((n_row,)),
             dma((n_row,)),
             dma,
@@ -363,19 +360,26 @@
         store_in[0],
         store_out[0],
     )
-    half = width // HALVES
-    moved = pl.pallas_call(
+    moved, grad = pl.pallas_call(
         merge_kernel,
-        out_shape=jax.ShapeDtypeStruct((tokens, width), BF16),
-        grid=(HALVES,),
+        out_shape=(
+            jax.ShapeDtypeStruct((tokens, width), BF16),
+            jax.ShapeDtypeStruct((top, tokens), F32),
+        ),
+        grid=(QUARTERS,),
         in_specs=[
-            pl.BlockSpec((tokens, half), lambda h: (0, h)),
-            pl.BlockSpec((1, ROWS, band), lambda h: (h, 0, 0)),
-            pl.BlockSpec((8, tokens), lambda h: (0, 0)),
+            pl.BlockSpec((tokens, quarter), lambda q: (0, q)),
+            pl.BlockSpec((1, ROWS, band), lambda q: (q, 0, 0)),
+            pl.BlockSpec((8, tokens), lambda q: (0, 0)),
+            pl.BlockSpec((top, tokens), lambda q: (0, 0)),
         ],
-        out_specs=pl.BlockSpec((tokens, half), lambda h: (0, h)),
+        out_specs=(
+            pl.BlockSpec((tokens, quarter), lambda q: (0, q)),
+            pl.BlockSpec((top, tokens), lambda q: (0, 0)),
+        ),
+        scratch_shapes=[pltpu.VMEM((CAP, tokens, band), F32)],
         name="merge",
-    )(shift, rows, scale)
+    )(shift, rows, scale, grad)
     return (moved[None], jnp.transpose(grad)[None])
 
 

time: 40.4 us -> 34.4 us (0.85)
  Pallas kernels: 37.8 us -> 32.9 us
  local copies, waits for them, and re-layouts: 1.22 us -> 0 us
    pallas_call x1, Pallas kernels: 35.3 us -> 29.2 us  [on_device(): pl.pallas_call(functools.partial(expert_kernel, n_row, n_sec), out_shape=...]
    pallas_call x1, Pallas kernels: 2.42 us -> 3.68 us  [on_device(): pl.pallas_call(merge_kernel, out_shape=(jax.ShapeDtypeStruct((tokens, wid...]
    unnamed x1 -> x0, local copies, waits for them, and re-layouts: 1.22 us -> none
where the time goes in v2:
time: 34.4 us; the launch traced here: 34.2 us
  Pallas kernels  32.9 us (96%)
  between operations  1.29 us (4%)
    pallas_call x1, Pallas kernels, on_device(): pl.pallas_call(functools.partial(expert_kernel, n_row, n_sec), out_shape=...  29.2 us
    pallas_call x1, Pallas kernels, on_device(): pl.pallas_call(merge_kernel, out_shape=(jax.ShapeDtypeStruct((tokens, wid...  3.68 us

profile of v2, /device:TPU:1, one launch (start us, length us, event | category | flops | bytes accessed | tf_op | source)
XLA Modules:
  0.0 34.2 jit_solution(7211046660068579885)
XLA Ops:
  1.3 29.2 %expert.1 = (bf16[128,4096]{1,0:T(8,128)(2,1)}, f32[4,16,128]{2,1,0:T(8,128)}, f32[8,128]{1,0:T(8,128)}, f32[2,128]{1,0:T(2,128)}) custom-call(s32[1]{0:T(128)S(6)} %copy.9.hot_ref, s32[2,128]{1,0:T(2,128)} %bitcast.18, f32[2,128]{1,0:T(2,128)} %bitcast.19, bf16[128,4096]{1,0:T(8,128)(2,1)} %bitcast.16, bf16[128,4096]{1,0:T(8,128)(2,1)} %bitcast.17, ...), custom_call_target="tpu_custom_call" | custom-call | flops 587202560 | bytes 22020096 | tf_op jit(solution)/shard_map/expert/pallas_call | solution.py:307
  30.5 3.7 %merge.1 = (bf16[128,4096]{1,0:T(8,128)(2,1)}, f32[2,128]{1,0:T(2,128)}) custom-call(bf16[128,4096]{1,0:T(8,128)(2,1)} %get-tuple-element.8.shift_ref, f32[4,16,128]{2,1,0:T(8,128)} %get-tuple-element.9.rows_ref, f32[8,128]{1,0:T(8,128)} %get-tuple-element.10.scale_ref, f32[2,128]{1,0:T(2,128)} %get-tuple-element.11.grad_ref), custom_call_target="tpu_custom_call" | custom-call | tf_op jit(solution)/shard_map/merge/pallas_call | solution.py:363

commit v3 on v2

--- a/solution.py
+++ b/solution.py
@@ -240,14 +240,21 @@
     @pl.when(has_next)
     def _():
         small.wait_recv()
-        scale_out[...] = scale_land[...]
+        diag = iota((tokens, tokens), 0) == iota((tokens, tokens), 1)
+        for j in range(CAP):
+            scale_out[:, j : j + 1] = jnp.sum(
+                jnp.where(diag, scale_land[j : j + 1, :], 0.0), axis=1, keepdims=True
+            )
         shift.wait_recv()
         for q in range(QUARTERS):
             @pl.loop(0, n_row)
             def _(r):
                 back_copy(q, r, r).wait_recv()
 
-            rows_out[q] = jnp.sum(land[q].astype(F32), axis=0).astype(BF16).astype(F32)
+            total = jnp.sum(land[q].astype(F32), axis=0).astype(BF16).astype(F32)
+            for b in range(BANDS):
+                at = q * quarter + b * band
+                rows_out[:, at : at + band] = total[b * CAP : (b + 1) * CAP]
 
     @pl.when(jnp.logical_not(has_next))
     def _():
@@ -271,26 +278,6 @@
         def _(r):
             for q in range(QUARTERS):
                 back_copy(q, r, me).wait_send()
-
-
-def merge_kernel(shift_ref, rows_ref, scale_ref, grad_ref, out_ref, grad_out, cols):
-    tokens = shift_ref.shape[0]
-    band = rows_ref.shape[2]
-
-    @pl.when(pl.program_id(0) == 0)
-    def _():
-        grad_out[...] = grad_ref[...]
-        diag = iota((tokens, tokens), 0) == iota((tokens, tokens), 1)
-        for j in range(CAP):
-            col = jnp.sum(jnp.where(diag, scale_ref[j : j + 1, :], 0.0), axis=1, keepdims=True)
-            cols[j] = jnp.broadcast_to(col, (tokens, band))
-
-    for b in range(BANDS):
-        at = slice(b * band, (b + 1) * band)
-        value = shift_ref[:, at].astype(F32)
-        for j in range(CAP):
-            value = value + cols[j] * rows_ref[0, b * CAP + j : b * CAP + j + 1, :]
-        out_ref[:, at] = value.astype(BF16)
 
 
 def on_device(n_row, n_sec, layer_input, cotangent, route_weight, chosen, hot_expert, store_in, store_out):
@@ -307,13 +294,13 @@
     shift, rows, scale, grad = pl.pallas_call(
         functools.partial(expert_kernel, n_row, n_sec),
         out_shape=(
-            jax.ShapeDtypeStruct((tokens, width), BF16),
-            jax.ShapeDtypeStruct((QUARTERS, ROWS, band), F32),
-            jax.ShapeDtypeStruct((8, tokens), F32),
-            jax.ShapeDtypeStruct((top, tokens), F32),
+            pltpu.VMEM((tokens, width), BF16),
+            pltpu.VMEM((CAP, width), F32),
+            pltpu.VMEM((tokens, CAP), F32),
+            pltpu.VMEM((top, tokens), F32),
         ),
         in_specs=[pl.BlockSpec(memory_space=pltpu.SMEM), vmem, vmem, hbm, hbm, hbm, hbm],
-        out_specs=(hbm, vmem, vmem, vmem),
+        out_specs=(vmem, vmem, vmem, vmem),
         scratch_shapes=[
             pltpu.VMEM((tokens, width), BF16),
             pltpu.VMEM((tokens, width), BF16),
@@ -360,26 +347,10 @@
         store_in[0],
         store_out[0],
     )
-    moved, grad = pl.pallas_call(
-        merge_kernel,
-        out_shape=(
-            jax.ShapeDtypeStruct((tokens, width), BF16),
-            jax.ShapeDtypeStruct((top, tokens), F32),
-        ),
-        grid=(QUARTERS,),
-        in_specs=[
-            pl.BlockSpec((tokens, quarter), lambda q: (0, q)),
-            pl.BlockSpec((1, ROWS, band), lambda q: (q, 0, 0)),
-            pl.BlockSpec((8, tokens), lambda q: (0, 0)),
-            pl.BlockSpec((top, tokens), lambda q: (0, 0)),
-        ],
-        out_specs=(
-            pl.BlockSpec((tokens, quarter), lambda q: (0, q)),
-            pl.BlockSpec((top, tokens), lambda q: (0, 0)),
-        ),
-        scratch_shapes=[pltpu.VMEM((CAP, tokens, band), F32)],
-        name="merge",
-    )(shift, rows, scale, grad)
+    moved = shift.astype(F32)
+    for j in range(CAP):
+        moved = moved + scale[:, j : j + 1] * rows[j : j + 1]
+    moved = moved.astype(BF16)
     return (moved[None], jnp.transpose(grad)[None])
 
 

time: 34.4 us -> 32.3 us (0.939)
  Pallas kernels: 32.9 us -> 28.6 us
  other arithmetic: 0 us -> 1.43 us
  local copies, waits for them, and re-layouts: 0 us -> 0.77 us
    pallas_call x1 -> x0, Pallas kernels: 3.68 us -> none  [on_device(): pl.pallas_call(merge_kernel, out_shape=(jax.ShapeDtypeStruct((tokens, wid...]
    broadcast_in_dim x0 -> x1, other arithmetic: none -> 1.43 us  [on_device(): return (moved[None], jnp.transpose(grad)[None])]
    pallas_call x1, Pallas kernels: 29.2 us -> 28.6 us  [on_device(): pl.pallas_call(functools.partial(expert_kernel, n_row, n_sec), out_shape=...]
    unnamed x0 -> x1, local copies, waits for them, and re-layouts: none -> 0.56 us
where the time goes in v3:
time: 32.3 us; the launch traced here: 32.1 us
  Pallas kernels  28.6 us (89%)
  other arithmetic  1.43 us (4%)
  between operations  1.3 us (4%)
  local copies, waits for them, and re-layouts  0.77 us (2%)
    pallas_call x1, Pallas kernels, on_device(): pl.pallas_call(functools.partial(expert_kernel, n_row, n_sec), out_shape=...  28.6 us
    broadcast_in_dim x1, other arithmetic, on_device(): return (moved[None], jnp.transpose(grad)[None])  1.43 us

profile of v3, /device:TPU:1, one launch (start us, length us, event | category | flops | bytes accessed | tf_op | source)
XLA Modules:
  0.0 32.1 jit_solution(3879220054043063821)
XLA Ops:
  1.3 28.6 %expert.1 = (bf16[128,4096]{1,0:T(8,128)(2,1)S(1)}, f32[2,4096]{1,0:T(2,128)S(1)}, f32[128,2]{1,0:T(8,128)S(1)}, f32[2,128]{1,0:T(2,128)S(1)}) custom-call(s32[1]{0:T(128)S(6)} %copy.11.hot_ref, s32[2,128]{1,0:T(2,128)} %bitcast.24, f32[2,128]{1,0:T(2,128)} %bitcast.25, bf16[128,4096]{1,0:T(8,128)(2,1)} %bitcast.20, bf16[128,4096]{1,0:T(8,128)(2,1)} %bitcast.21, ...), custom_call_target="tpu_custom_call" | custom-call | flops 587202560 | bytes 22020096 | tf_op jit(solution)/shard_map/expert/pallas_call | solution.py:294
  29.9 0.6 %copy.10 = f32[1,128,2]{1,2,0:T(2,128)} copy(f32[1,128,2]{1,2,0:T(2,128)S(1)} %bitcast.17) | data formatting | bytes 2048
  30.5 0.2 slice_reduce_fusion.1
  30.7 1.4 %fusion = bf16[1,128,4096]{2,1,0:T(8,128)(2,1)} fusion(bf16[128,4096]{1,0:T(8,128)(2,1)S(1)} %get-tuple-element.6, f32[4096]{0:T(1024)S(1)} %bitcast.23, f32[128]{0:T(128)S(1)} %get-tuple-element.11, f32[4096]{0:T(1024)S(1)} %bitcast.22, f32[128]{0:T(128)S(1)} %get-tuple-element.10), kind=kLoop, calls=%fused_computation.1 | loop fusion | flops 3145728 | bytes 2130944 | tf_op jit(solution)/shard_map/broadcast_in_dim | solution.py:354
  (1 shorter events, 0.0 us)

commit v4 on v3

--- a/solution.py
+++ b/solution.py
@@ -15,6 +15,7 @@
 BANDS = ROWS // CAP
 QUARTERS = 4
 LAST = (((1,), (1,)), ((), ()))
+FIRST = (((0,), (1,)), ((), ()))
 
 
 def iota(shape, dim):
@@ -25,9 +26,9 @@
     n_row, n_sec, hot_ref, chosen_ref, weight_ref, x_hbm, cot_hbm, win_hbm, wout_hbm,
     shift_out, rows_out, scale_out, grad_out,
     x_v, cot_v, win_v, wout_v, gath, xs, gs, pack, land,
-    scale_v, scale_land, score_v, score_land, zero_v,
+    scale_v, scale_land, score_v, score_land,
     win_sem, wout_sem, t_sem, gath_send, gath_recv, back_send, back_recv, score_send, score_recv,
-    small_send, small_recv, shift_send, shift_recv, zero_sem,
+    small_send, small_recv, shift_send, shift_recv,
 ):
     sec = lax.axis_index("section")
     me = lax.axis_index("row")
@@ -100,10 +101,17 @@
             )
         return block.astype(BF16)
 
-    def gath_copy(k, to, slot_of):
-        return pltpu.make_async_remote_copy(
-            gath.at[k, slot_of], gath.at[k, slot_of], gath_send.at[k, to], gath_recv.at[k, slot_of],
-            device_id={"section": sec, "row": to}, device_id_type=MESH,
+    def gath_copy(k, i):
+        return pltpu.make_async_remote_copy(
+            gath.at[k, 0], gath.at[k, i], gath_send.at[k], gath_recv.at[k],
+            device_id={"section": sec, "row": lax.rem(me + n_row - i, n_row)}, device_id_type=MESH,
+        )
+
+    def gath_all(k):
+        others = gath.at[k, pl.ds(1, n_row - 1)]
+        return pltpu.make_async_remote_copy(
+            others, others, gath_send.at[k], gath_recv.at[k],
+            device_id={"section": sec, "row": me}, device_id_type=MESH,
         )
 
     prev = {"section": sec - 1, "row": me}
@@ -113,17 +121,16 @@
     small = pltpu.make_async_remote_copy(
         scale_v, scale_land, small_send, small_recv, device_id=prev, device_id_type=MESH
     )
-    blank = pltpu.make_async_copy(zero_v, shift_out, zero_sem)
 
     x_copy.wait()
-    gath[0, pl.ds(me, 1)] = held_rows(x_v)[None]
+    gath[0, 0] = held_rows(x_v)
 
     sides = has_prev.astype(jnp.int32) + has_next.astype(jnp.int32)
     pl.semaphore_wait(barrier, n_row - 1 + n_row * sides)
 
     @pl.loop(1, n_row)
     def _(i):
-        gath_copy(0, lax.rem(me + i, n_row), me).start()
+        gath_copy(0, i).start()
 
     cot_copy.wait()
     for c in range(QUARTERS):
@@ -131,33 +138,25 @@
         win_copy(1, c).start()
     wout_copy.start()
 
-    gath[1, pl.ds(me, 1)] = held_rows(cot_v)[None]
+    gath[1, 0] = held_rows(cot_v)
 
     @pl.loop(1, n_row)
     def _(i):
-        gath_copy(1, lax.rem(me + i, n_row), me).start()
+        gath_copy(1, i).start()
 
     @pl.when(has_prev)
     def _():
         shift.start()
         small.start()
 
-    @pl.when(jnp.logical_not(has_next))
-    def _():
-        zero_v[...] = jnp.zeros_like(zero_v)
-        blank.start()
-
     to_row = iota((BANDS * slots, n_row * ROWS), 0)
     slot = lax.rem(to_row, slots)
-    want = (slot // CAP) * ROWS + (to_row // slots) * CAP + lax.rem(slot, CAP)
+    away = lax.rem(slot // CAP - me + n_row, n_row)
+    want = away * ROWS + (to_row // slots) * CAP + lax.rem(slot, CAP)
     spread = (iota((BANDS * slots, n_row * ROWS), 1) == want).astype(BF16)
 
     def gathered(k, rows_ref):
-        @pl.loop(1, n_row)
-        def _(i):
-            src = lax.rem(me + i, n_row)
-            gath_copy(k, src, src).wait_recv()
-
+        gath_all(k).wait_recv()
         everyone = gath[k].reshape(n_row * ROWS, part)
         rows = jnp.dot(spread, everyone, preferred_element_type=F32).astype(BF16)
         for c in range(BANDS):
@@ -169,11 +168,12 @@
         cols = slice(c * quarter, (c + 1) * quarter)
         win_copy(0, c).wait()
         win_copy(1, c).wait()
-        g_part = jnp.dot(xs[:, cols], win_v[0, cols, :], preferred_element_type=F32)
-        u_part = jnp.dot(xs[:, cols], win_v[1, cols, :], preferred_element_type=F32)
+        g_part = lax.dot_general(win_v[0, cols, :], xs[:, cols], FIRST, preferred_element_type=F32)
+        u_part = lax.dot_general(win_v[1, cols, :], xs[:, cols], FIRST, preferred_element_type=F32)
         gate = g_part if gate is None else gate + g_part
         up = u_part if up is None else up + u_part
 
+    gate, up = gate.T, up.T
     gathered(1, gs)
     wout_copy.wait()
     dh = lax.dot_general(wout_v[...], gs[...], LAST, preferred_element_type=F32).T
@@ -187,22 +187,35 @@
     score_row = jnp.sum(jnp.where(diag, score, 0.0), axis=0, keepdims=True)
     score_v[...] = jnp.broadcast_to(score_row, score_v.shape)
 
-    def score_copy(to, slot_of):
-        return pltpu.make_async_remote_copy(
-            score_v, score_land.at[slot_of], score_send.at[to], score_recv.at[slot_of],
-            device_id={"section": sec, "row": to}, device_id_type=MESH,
+    score_land[0] = score_v[...]
+
+    def score_copy(i):
+        return pltpu.make_async_remote_copy(
+            score_v, score_land.at[i], score_send, score_recv,
+            device_id={"section": sec, "row": lax.rem(me + n_row - i, n_row)}, device_id_type=MESH,
+        )
+
+    def score_all():
+        others = score_land.at[pl.ds(1, n_row - 1)]
+        return pltpu.make_async_remote_copy(
+            others, others, score_send, score_recv,
+            device_id={"section": sec, "row": me}, device_id_type=MESH,
         )
 
     @pl.loop(1, n_row)
     def _(i):
-        score_copy(lax.rem(me + i, n_row), me).start()
-
-    score_land[pl.ds(me, 1)] = score_v[...][None]
-
-    def back_copy(q, r, slot_of):
-        return pltpu.make_async_remote_copy(
-            pack.at[q, r], land.at[q, slot_of], back_send.at[q, r], back_recv.at[q, slot_of],
+        score_copy(i).start()
+
+    def back_copy(q, r):
+        return pltpu.make_async_remote_copy(
+            pack.at[q, r], land.at[q, me], back_send.at[q], back_recv.at[q],
             device_id={"section": sec - 1, "row": r}, device_id_type=MESH,
+        )
+
+    def back_all(q):
+        return pltpu.make_async_remote_copy(
+            pack.at[q], land.at[q], back_send.at[q], back_recv.at[q],
+            device_id={"section": sec - 1, "row": me}, device_id_type=MESH,
         )
 
     @pl.when(has_prev)
@@ -222,13 +235,9 @@
 
             @pl.loop(0, n_row)
             def _(r):
-                back_copy(q, r, me).start()
-
-    @pl.loop(1, n_row)
-    def _(i):
-        src = lax.rem(me + i, n_row)
-        score_copy(src, src).wait_recv()
-
+                back_copy(q, r).start()
+
+    score_all().wait_recv()
     sums = jnp.sum(score_land[...], axis=0)
     lane = iota(sums.shape, 1)
     grad_tok = jnp.zeros((1, tokens), F32)
@@ -237,47 +246,58 @@
         grad_tok = grad_tok + picks[j] * mine
     grad_out[...] = held * grad_tok
 
+    gath_all(0).wait_send()
+    gath_all(1).wait_send()
+    score_all().wait_send()
+
+    @pl.when(has_prev)
+    def _():
+        small.wait_send()
+        shift.wait_send()
+
     @pl.when(has_next)
     def _():
         small.wait_recv()
         diag = iota((tokens, tokens), 0) == iota((tokens, tokens), 1)
         for j in range(CAP):
-            scale_out[:, j : j + 1] = jnp.sum(
-                jnp.where(diag, scale_land[j : j + 1, :], 0.0), axis=1, keepdims=True
-            )
+            col = jnp.sum(jnp.where(diag, scale_land[j : j + 1, :], 0.0), axis=1, keepdims=True)
+            scale_out[j] = jnp.broadcast_to(col, (tokens, band))
         shift.wait_recv()
         for q in range(QUARTERS):
-            @pl.loop(0, n_row)
-            def _(r):
-                back_copy(q, r, r).wait_recv()
-
-            total = jnp.sum(land[q].astype(F32), axis=0).astype(BF16).astype(F32)
-            for b in range(BANDS):
-                at = q * quarter + b * band
-                rows_out[:, at : at + band] = total[b * CAP : (b + 1) * CAP]
+            back_all(q).wait_recv()
+            rows_out[q] = jnp.sum(land[q].astype(F32), axis=0).astype(BF16).astype(F32)
 
     @pl.when(jnp.logical_not(has_next))
     def _():
         rows_out[...] = jnp.zeros_like(rows_out)
         scale_out[...] = jnp.zeros_like(scale_out)
-        blank.wait()
-
-    @pl.loop(1, n_row)
-    def _(i):
-        to = lax.rem(me + i, n_row)
-        gath_copy(0, to, me).wait_send()
-        gath_copy(1, to, me).wait_send()
-        score_copy(to, me).wait_send()
+        shift_out[...] = jnp.zeros_like(shift_out)
 
     @pl.when(has_prev)
     def _():
-        shift.wait_send()
-        small.wait_send()
-
-        @pl.loop(0, n_row)
-        def _(r):
-            for q in range(QUARTERS):
-                back_copy(q, r, me).wait_send()
+        for q in range(QUARTERS):
+            back_all(q).wait_send()
+
+
+def merge_kernel(shift_ref, rows_ref, scale_ref, grad_ref, out_hbm, grad_hbm, out_v, sem):
+    quarters, _, band = rows_ref.shape
+    quarter = band * BANDS
+    grad_copy = pltpu.make_async_copy(grad_ref, grad_hbm, sem.at[quarters])
+    grad_copy.start()
+    copies = []
+    for q in range(quarters):
+        for b in range(BANDS):
+            at = slice(q * quarter + b * band, q * quarter + (b + 1) * band)
+            value = shift_ref[:, at].astype(F32)
+            for j in range(CAP):
+                value = value + scale_ref[j] * rows_ref[q, b * CAP + j : b * CAP + j + 1, :]
+            out_v[:, at] = value.astype(BF16)
+        cols = pl.ds(q * quarter, quarter)
+        copies.append(pltpu.make_async_copy(out_v.at[:, cols], out_hbm.at[:, cols], sem.at[q]))
+        copies[-1].start()
+    for copy in copies:
+        copy.wait()
+    grad_copy.wait()
 
 
 def on_device(n_row, n_sec, layer_input, cotangent, route_weight, chosen, hot_expert, store_in, store_out):
@@ -295,8 +315,8 @@
         functools.partial(expert_kernel, n_row, n_sec),
         out_shape=(
             pltpu.VMEM((tokens, width), BF16),
-            pltpu.VMEM((CAP, width), F32),
-            pltpu.VMEM((tokens, CAP), F32),
+            pltpu.VMEM((QUARTERS, ROWS, band), F32),
+            pltpu.VMEM((CAP, tokens, band), F32),
             pltpu.VMEM((top, tokens), F32),
         ),
         in_specs=[pl.BlockSpec(memory_space=pltpu.SMEM), vmem, vmem, hbm, hbm, hbm, hbm],
@@ -315,16 +335,14 @@
             pltpu.VMEM((8, tokens), F32),
             pltpu.VMEM((8, 128), F32),
             pltpu.VMEM((n_row, 8, 128), F32),
-            pltpu.VMEM((tokens, width), BF16),
             dma((2, QUARTERS)),
             dma,
             dma((2,)),
-            dma((2, n_row)),
-            dma((2, n_row)),
-            dma((QUARTERS, n_row)),
-            dma((QUARTERS, n_row)),
-            dma((n_row,)),
-            dma((n_row,)),
+            dma((2,)),
+            dma((2,)),
+            dma((QUARTERS,)),
+            dma((QUARTERS,)),
+            dma,
             dma,
             dma,
             dma,
@@ -347,10 +365,17 @@
         store_in[0],
         store_out[0],
     )
-    moved = shift.astype(F32)
-    for j in range(CAP):
-        moved = moved + scale[:, j : j + 1] * rows[j : j + 1]
-    moved = moved.astype(BF16)
+    moved, grad = pl.pallas_call(
+        merge_kernel,
+        out_shape=(
+            jax.ShapeDtypeStruct((tokens, width), BF16),
+            jax.ShapeDtypeStruct((top, tokens), F32),
+        ),
+        in_specs=[vmem] * 4,
+        out_specs=(hbm, hbm),
+        scratch_shapes=[pltpu.VMEM((tokens, width), BF16), dma((QUARTERS + 1,))],
+        name="merge",
+    )(shift, rows, scale, grad)
     return (moved[None], jnp.transpose(grad)[None])
 
 

time: 32.3 us -> 39.2 us (1.21)
  Pallas kernels: 28.6 us -> 34.9 us
  local copies, waits for them, and re-layouts: 0.77 us -> 2.76 us
  other arithmetic: 1.43 us -> 0 us
    pallas_call x1, Pallas kernels: 28.6 us -> 32.5 us  [on_device(): pl.pallas_call(functools.partial(expert_kernel, n_row, n_sec), out_shape=...]
    pallas_call x0 -> x1, Pallas kernels: none -> 2.41 us  [on_device(): pl.pallas_call(merge_kernel, out_shape=(jax.ShapeDtypeStruct((tokens, wid...]
    unnamed x1 -> x8, local copies, waits for them, and re-layouts: 0.56 us -> 2.76 us
    broadcast_in_dim x1 -> x0, other arithmetic: 1.43 us -> none  [on_device(): return (moved[None], jnp.transpose(grad)[None])]
where the time goes in v4:
time: 39.2 us; the launch traced here: 39 us
  Pallas kernels  34.9 us (89%)
  local copies, waits for them, and re-layouts  2.76 us (7%)
  between operations  1.3 us (3%)
    pallas_call x1, Pallas kernels, on_device(): pl.pallas_call(functools.partial(expert_kernel, n_row, n_sec), out_shape=...  32.5 us
    unnamed x8, local copies, waits for them, and re-layouts  2.76 us
    pallas_call x1, Pallas kernels, on_device(): pl.pallas_call(merge_kernel, out_shape=(jax.ShapeDtypeStruct((tokens, wid...  2.41 us

profile of v4, /device:TPU:1, one launch (start us, length us, event | category | flops | bytes accessed | tf_op | source)
XLA Modules:
  0.0 39.0 jit_solution(2340809243176358021)
XLA Ops:
  1.3 32.5 %expert.1 = (bf16[128,4096]{1,0:T(8,128)(2,1)S(1)}, f32[4,16,128]{2,1,0:T(8,128)S(1)}, f32[2,128,128]{2,1,0:T(8,128)S(1)}, f32[2,128]{1,0:T(2,128)S(1)}) custom-call(s32[1]{0:T(128)S(6)} %copy.9.hot_ref, s32[2,128]{1,0:T(2,128)} %bitcast.18, f32[2,128]{1,0:T(2,128)} %bitcast.19, bf16[128,4096]{1,0:T(8,128)(2,1)} %bitcast.16, bf16[128,4096]{1,0:T(8,128)(2,1)} %bitcast.17, ...), custom_call_target="tpu_custom_call" | custom-call | flops 587202560 | bytes 22020096 | tf_op jit(solution)/shard_map/expert/pallas_call | solution.py:314
  33.8 0.0 copy-start
  33.8 1.0 %copy-done = bf16[128,4096]{1,0:T(8,128)(2,1)} copy-done((bf16[128,4096]{1,0:T(8,128)(2,1)}, bf16[128,4096]{1,0:T(8,128)(2,1)S(1)}, u32[]{:S(2)}) %copy-start) | copy-done | bytes 1048600
  34.8 0.0 copy-start.1
  34.8 0.6 %copy-done.1 = f32[2,128,128]{2,1,0:T(8,128)} copy-done((f32[2,128,128]{2,1,0:T(8,128)}, f32[2,128,128]{2,1,0:T(8,128)S(1)}, u32[]{:S(2)}) %copy-start.1) | copy-done | bytes 131096
  35.4 0.0 copy-start.2
  35.4 0.6 %copy-done.2 = f32[4,16,128]{2,1,0:T(8,128)} copy-done((f32[4,16,128]{2,1,0:T(8,128)}, f32[4,16,128]{2,1,0:T(8,128)S(1)}, u32[]{:S(2)}) %copy-start.2) | copy-done | bytes 32792
  36.0 0.0 copy-start.3
  36.0 0.5 %copy-done.3 = f32[2,128]{1,0:T(2,128)} copy-done((f32[2,128]{1,0:T(2,128)}, f32[2,128]{1,0:T(2,128)S(1)}, u32[]{:S(2)}) %copy-start.3) | copy-done | bytes 1048
  36.6 2.4 %merge.1 = (bf16[128,4096]{1,0:T(8,128)(2,1)}, f32[2,128]{1,0:T(2,128)}) custom-call(bf16[128,4096]{1,0:T(8,128)(2,1)} %copy-done, f32[4,16,128]{2,1,0:T(8,128)} %copy-done.2, f32[2,128,128]{2,1,0:T(8,128)} %copy-done.1, f32[2,128]{1,0:T(2,128)} %copy-done.3), custom_call_target="tpu_custom_call" | custom-call | tf_op jit(solution)/shard_map/merge/pallas_call | solution.py:368
Async XLA Ops:
  33.8 1.0 %copy-start = (bf16[128,4096]{1,0:T(8,128)(2,1)}, bf16[128,4096]{1,0:T(8,128)(2,1)S(1)}, u32[]{:S(2)}) copy-start(bf16[128,4096]{1,0:T(8,128)(2,1)S(1)} %get-tuple-element.8.shift_ref) | copy-start | bytes 3145732
  34.8 0.6 %copy-start.1 = (f32[2,128,128]{2,1,0:T(8,128)}, f32[2,128,128]{2,1,0:T(8,128)S(1)}, u32[]{:S(2)}) copy-start(f32[2,128,128]{2,1,0:T(8,128)S(1)} %get-tuple-element.10.scale_ref) | copy-start | bytes 393220
  35.4 0.6 %copy-start.2 = (f32[4,16,128]{2,1,0:T(8,128)}, f32[4,16,128]{2,1,0:T(8,128)S(1)}, u32[]{:S(2)}) copy-start(f32[4,16,128]{2,1,0:T(8,128)S(1)} %get-tuple-element.9.rows_ref) | copy-start | bytes 98308
  36.0 0.5 %copy-start.3 = (f32[2,128]{1,0:T(2,128)}, f32[2,128]{1,0:T(2,128)S(1)}, u32[]{:S(2)}) copy-start(f32[2,128]{1,0:T(2,128)S(1)} %get-tuple-element.11.grad_ref) | copy-start | bytes 3076

commit v5 on v4

--- a/solution.py
+++ b/solution.py
@@ -14,8 +14,8 @@
 ROWS = 16
 BANDS = ROWS // CAP
 QUARTERS = 4
+HALVES = 2
 LAST = (((1,), (1,)), ((), ()))
-FIRST = (((0,), (1,)), ((), ()))
 
 
 def iota(shape, dim):
@@ -24,7 +24,7 @@
 
 def expert_kernel(
     n_row, n_sec, hot_ref, chosen_ref, weight_ref, x_hbm, cot_hbm, win_hbm, wout_hbm,
-    shift_out, rows_out, scale_out, grad_out,
+    moved_out, grad_out,
     x_v, cot_v, win_v, wout_v, gath, xs, gs, pack, land,
     scale_v, scale_land, score_v, score_land,
     win_sem, wout_sem, t_sem, gath_send, gath_recv, back_send, back_recv, score_send, score_recv,
@@ -34,7 +34,8 @@
     me = lax.axis_index("row")
     tokens, width = x_v.shape
     slots = n_row * CAP
-    part = width // BANDS
+    half = width // HALVES
+    part = half // BANDS
     quarter = width // QUARTERS
     band = quarter // BANDS
 
@@ -43,10 +44,13 @@
         return pltpu.make_async_copy(win_hbm.at[i, rows], win_v.at[i, rows], win_sem.at[i, c])
 
     wout_copy = pltpu.make_async_copy(wout_hbm, wout_v, wout_sem)
-    x_copy = pltpu.make_async_copy(x_hbm, x_v, t_sem.at[0])
-    cot_copy = pltpu.make_async_copy(cot_hbm, cot_v, t_sem.at[1])
-    x_copy.start()
-    cot_copy.start()
+    def token_copy(k):
+        source, to = ((x_hbm, x_v), (cot_hbm, cot_v))[k // HALVES]
+        cols = pl.ds(k % HALVES * half, half)
+        return pltpu.make_async_copy(source.at[:, cols], to.at[:, cols], t_sem.at[k])
+
+    for k in range(2 * HALVES):
+        token_copy(k).start()
 
     has_prev = sec > 0
     has_next = sec < n_sec - 1
@@ -93,13 +97,18 @@
             one = one + jnp.where(lead == c * CAP + j, picks[j], 0.0)
         ones.append(one.astype(BF16))
 
-    def held_rows(source):
+    def held_rows(k):
+        source = (x_v, cot_v)[k // HALVES]
         block = jnp.zeros((ROWS, part), F32)
         for c in range(BANDS):
-            block = block + jnp.dot(
-                ones[c], source[:, c * part : (c + 1) * part], preferred_element_type=F32
-            )
-        return block.astype(BF16)
+            at = k % HALVES * half + c * part
+            block = block + jnp.dot(ones[c], source[:, at : at + part], preferred_element_type=F32)
+        gath[k, 0] = block.astype(BF16)
+
+    def send_rows(k):
+        @pl.loop(1, n_row)
+        def _(i):
+            gath_copy(k, i).start()
 
     def gath_copy(k, i):
         return pltpu.make_async_remote_copy(
@@ -116,33 +125,31 @@
 
     prev = {"section": sec - 1, "row": me}
     shift = pltpu.make_async_remote_copy(
-        cot_hbm, shift_out, shift_send, shift_recv, device_id=prev, device_id_type=MESH
+        cot_hbm, moved_out, shift_send, shift_recv, device_id=prev, device_id_type=MESH
     )
     small = pltpu.make_async_remote_copy(
         scale_v, scale_land, small_send, small_recv, device_id=prev, device_id_type=MESH
     )
 
-    x_copy.wait()
-    gath[0, 0] = held_rows(x_v)
-
+    token_copy(0).wait()
+    held_rows(0)
     sides = has_prev.astype(jnp.int32) + has_next.astype(jnp.int32)
     pl.semaphore_wait(barrier, n_row - 1 + n_row * sides)
-
-    @pl.loop(1, n_row)
-    def _(i):
-        gath_copy(0, i).start()
-
-    cot_copy.wait()
+    send_rows(0)
+    token_copy(1).wait()
+    held_rows(1)
+    send_rows(1)
+
+    for k in range(HALVES, 2 * HALVES):
+        token_copy(k).wait()
     for c in range(QUARTERS):
         win_copy(0, c).start()
         win_copy(1, c).start()
     wout_copy.start()
 
-    gath[1, 0] = held_rows(cot_v)
-
-    @pl.loop(1, n_row)
-    def _(i):
-        gath_copy(1, i).start()
+    for k in range(HALVES, 2 * HALVES):
+        held_rows(k)
+        send_rows(k)
 
     @pl.when(has_prev)
     def _():
@@ -155,26 +162,28 @@
     want = away * ROWS + (to_row // slots) * CAP + lax.rem(slot, CAP)
     spread = (iota((BANDS * slots, n_row * ROWS), 1) == want).astype(BF16)
 
-    def gathered(k, rows_ref):
+    def gathered(k, rows_ref, h):
         gath_all(k).wait_recv()
         everyone = gath[k].reshape(n_row * ROWS, part)
         rows = jnp.dot(spread, everyone, preferred_element_type=F32).astype(BF16)
         for c in range(BANDS):
-            rows_ref[:, c * part : (c + 1) * part] = rows[c * slots : (c + 1) * slots]
-
-    gathered(0, xs)
+            at = h * half + c * part
+            rows_ref[:, at : at + part] = rows[c * slots : (c + 1) * slots]
+
     gate = up = None
     for c in range(QUARTERS):
         cols = slice(c * quarter, (c + 1) * quarter)
+        if c % (QUARTERS // HALVES) == 0:
+            gathered(c // (QUARTERS // HALVES), xs, c // (QUARTERS // HALVES))
         win_copy(0, c).wait()
         win_copy(1, c).wait()
-        g_part = lax.dot_general(win_v[0, cols, :], xs[:, cols], FIRST, preferred_element_type=F32)
-        u_part = lax.dot_general(win_v[1, cols, :], xs[:, cols], FIRST, preferred_element_type=F32)
+        g_part = jnp.dot(xs[:, cols], win_v[0, cols, :], preferred_element_type=F32)
+        u_part = jnp.dot(xs[:, cols], win_v[1, cols, :], preferred_element_type=F32)
         gate = g_part if gate is None else gate + g_part
         up = u_part if up is None else up + u_part
 
-    gate, up = gate.T, up.T
-    gathered(1, gs)
+    gathered(2, gs, 0)
+    gathered(3, gs, 1)
     wout_copy.wait()
     dh = lax.dot_general(wout_v[...], gs[...], LAST, preferred_element_type=F32).T
 
@@ -234,8 +243,8 @@
             pack[q] = packed.reshape(n_row, ROWS, band)
 
             @pl.loop(0, n_row)
-            def _(r):
-                back_copy(q, r).start()
+            def _(i):
+                back_copy(q, lax.rem(me + i, n_row)).start()
 
     score_all().wait_recv()
     sums = jnp.sum(score_land[...], axis=0)
@@ -246,8 +255,8 @@
         grad_tok = grad_tok + picks[j] * mine
     grad_out[...] = held * grad_tok
 
-    gath_all(0).wait_send()
-    gath_all(1).wait_send()
+    for k in range(2 * HALVES):
+        gath_all(k).wait_send()
     score_all().wait_send()
 
     @pl.when(has_prev)
@@ -259,45 +268,29 @@
     def _():
         small.wait_recv()
         diag = iota((tokens, tokens), 0) == iota((tokens, tokens), 1)
+        scales = []
         for j in range(CAP):
             col = jnp.sum(jnp.where(diag, scale_land[j : j + 1, :], 0.0), axis=1, keepdims=True)
-            scale_out[j] = jnp.broadcast_to(col, (tokens, band))
+            scales.append(jnp.broadcast_to(col, (tokens, band)))
         shift.wait_recv()
         for q in range(QUARTERS):
             back_all(q).wait_recv()
-            rows_out[q] = jnp.sum(land[q].astype(F32), axis=0).astype(BF16).astype(F32)
+            rows = jnp.sum(land[q].astype(F32), axis=0).astype(BF16).astype(F32)
+            for b in range(BANDS):
+                at = slice(q * quarter + b * band, q * quarter + (b + 1) * band)
+                value = moved_out[:, at].astype(F32)
+                for j in range(CAP):
+                    value = value + scales[j] * rows[b * CAP + j : b * CAP + j + 1, :]
+                moved_out[:, at] = value.astype(BF16)
 
     @pl.when(jnp.logical_not(has_next))
     def _():
-        rows_out[...] = jnp.zeros_like(rows_out)
-        scale_out[...] = jnp.zeros_like(scale_out)
-        shift_out[...] = jnp.zeros_like(shift_out)
+        moved_out[...] = jnp.zeros_like(moved_out)
 
     @pl.when(has_prev)
     def _():
         for q in range(QUARTERS):
             back_all(q).wait_send()
-
-
-def merge_kernel(shift_ref, rows_ref, scale_ref, grad_ref, out_hbm, grad_hbm, out_v, sem):
-    quarters, _, band = rows_ref.shape
-    quarter = band * BANDS
-    grad_copy = pltpu.make_async_copy(grad_ref, grad_hbm, sem.at[quarters])
-    grad_copy.start()
-    copies = []
-    for q in range(quarters):
-        for b in range(BANDS):
-            at = slice(q * quarter + b * band, q * quarter + (b + 1) * band)
-            value = shift_ref[:, at].astype(F32)
-            for j in range(CAP):
-                value = value + scale_ref[j] * rows_ref[q, b * CAP + j : b * CAP + j + 1, :]
-            out_v[:, at] = value.astype(BF16)
-        cols = pl.ds(q * quarter, quarter)
-        copies.append(pltpu.make_async_copy(out_v.at[:, cols], out_hbm.at[:, cols], sem.at[q]))
-        copies[-1].start()
-    for copy in copies:
-        copy.wait()
-    grad_copy.wait()
 
 
 def on_device(n_row, n_sec, layer_input, cotangent, route_weight, chosen, hot_expert, store_in, store_out):
@@ -305,28 +298,27 @@
     ff = store_out.shape[1]
     top = chosen.shape[2]
     slots = n_row * CAP
-    part = width // BANDS
+    half = width // HALVES
+    part = half // BANDS
     quarter = width // QUARTERS
     band = quarter // BANDS
     hbm = pl.BlockSpec(memory_space=pl.ANY)
     vmem = pl.BlockSpec(memory_space=pltpu.VMEM)
     dma = pltpu.SemaphoreType.DMA
-    shift, rows, scale, grad = pl.pallas_call(
+    moved, grad = pl.pallas_call(
         functools.partial(expert_kernel, n_row, n_sec),
         out_shape=(
             pltpu.VMEM((tokens, width), BF16),
-            pltpu.VMEM((QUARTERS, ROWS, band), F32),
-            pltpu.VMEM((CAP, tokens, band), F32),
             pltpu.VMEM((top, tokens), F32),
         ),
         in_specs=[pl.BlockSpec(memory_space=pltpu.SMEM), vmem, vmem, hbm, hbm, hbm, hbm],
-        out_specs=(vmem, vmem, vmem, vmem),
+        out_specs=(vmem, vmem),
         scratch_shapes=[
             pltpu.VMEM((tokens, width), BF16),
             pltpu.VMEM((tokens, width), BF16),
             pltpu.VMEM((2, width, ff), BF16),
             pltpu.VMEM((ff, width), BF16),
-            pltpu.VMEM((2, n_row, ROWS, part), BF16),
+            pltpu.VMEM((2 * HALVES, n_row, ROWS, part), BF16),
             pltpu.VMEM((slots, width), BF16),
             pltpu.VMEM((slots, width), BF16),
             pltpu.VMEM((QUARTERS, n_row, ROWS, band), BF16),
@@ -337,9 +329,9 @@
             pltpu.VMEM((n_row, 8, 128), F32),
             dma((2, QUARTERS)),
             dma,
-            dma((2,)),
-            dma((2,)),
-            dma((2,)),
+            dma((2 * HALVES,)),
+            dma((2 * HALVES,)),
+            dma((2 * HALVES,)),
             dma((QUARTERS,)),
             dma((QUARTERS,)),
             dma,
@@ -365,17 +357,6 @@
         store_in[0],
         store_out[0],
     )
-    moved, grad = pl.pallas_call(
-        merge_kernel,
-        out_shape=(
-            jax.ShapeDtypeStruct((tokens, width), BF16),
-            jax.ShapeDtypeStruct((top, tokens), F32),
-        ),
-        in_specs=[vmem] * 4,
-        out_specs=(hbm, hbm),
-        scratch_shapes=[pltpu.VMEM((tokens, width), BF16), dma((QUARTERS + 1,))],
-        name="merge",
-    )(shift, rows, scale, grad)
     return (moved[None], jnp.transpose(grad)[None])
 
 

time: 39.2 us -> 30 us (0.77)
  Pallas kernels: 34.9 us -> 27 us
  local copies, waits for them, and re-layouts: 2.76 us -> 1.53 us
    pallas_call x1, Pallas kernels: 32.5 us -> 27 us  [on_device(): pl.pallas_call(functools.partial(expert_kernel, n_row, n_sec), out_shape=...]
    pallas_call x1 -> x0, Pallas kernels: 2.41 us -> none  [on_device(): pl.pallas_call(merge_kernel, out_shape=(jax.ShapeDtypeStruct((tokens, wid...]
    unnamed x8 -> x2, local copies, waits for them, and re-layouts: 2.76 us -> 1.53 us
where the time goes in v5:
time: 30 us; the launch traced here: 29.8 us
  Pallas kernels  27 us (90%)
  local copies, waits for them, and re-layouts  1.53 us (5%)
  between operations  1.29 us (4%)
    pallas_call x1, Pallas kernels, on_device(): pl.pallas_call(functools.partial(expert_kernel, n_row, n_sec), out_shape=...  27 us
    unnamed x2, local copies, waits for them, and re-layouts  1.53 us

profile of v5, /device:TPU:1, one launch (start us, length us, event | category | flops | bytes accessed | tf_op | source)
XLA Modules:
  0.0 29.8 jit_solution(6476159945368442027)
XLA Ops:
  1.3 27.0 %expert.1 = (bf16[128,4096]{1,0:T(8,128)(2,1)S(1)}, f32[2,128]{1,0:T(2,128)S(1)}) custom-call(s32[1]{0:T(128)S(6)} %copy.13.hot_ref, s32[2,128]{1,0:T(2,128)} %bitcast.20, f32[2,128]{1,0:T(2,128)} %bitcast.21, bf16[128,4096]{1,0:T(8,128)(2,1)} %bitcast.18, bf16[128,4096]{1,0:T(8,128)(2,1)} %bitcast.19, bf16[2,4096,896]{2,1,0:T(8,128)(2,1)} %bitcast.16, ...), custom_call_target="tpu_custom_call" | custom-call | flops 587202560 | bytes 22020096 | tf_op jit(solution)/shard_map/expert/pallas_call | solution.py:308
  28.3 1.0 %copy.11 = bf16[1,128,4096]{2,1,0:T(8,128)(2,1)} copy(bf16[1,128,4096]{2,1,0:T(8,128)(2,1)S(1)} %bitcast.14) | data formatting | bytes 2097152
  29.3 0.6 %copy.12 = f32[1,128,2]{1,2,0:T(2,128)} copy(f32[1,128,2]{1,2,0:T(2,128)S(1)} %bitcast.15) | data formatting | bytes 2048

commit v6 on v5

--- a/solution.py
+++ b/solution.py
@@ -23,16 +23,17 @@
 
 
 def expert_kernel(
-    n_row, n_sec, hot_ref, chosen_ref, weight_ref, x_hbm, cot_hbm, win_hbm, wout_hbm,
+    n_row, n_sec, hot_ref, chosen_hbm, weight_hbm, x_hbm, cot_hbm, win_hbm, wout_hbm,
     moved_out, grad_out,
-    x_v, cot_v, win_v, wout_v, gath, xs, gs, pack, land,
+    chosen_ref, weight_ref, x_v, cot_v, win_v, wout_v, gath, xs, gs, pack, land,
     scale_v, scale_land, score_v, score_land,
-    win_sem, wout_sem, t_sem, gath_send, gath_recv, back_send, back_recv, score_send, score_recv,
+    win_sem, wout_sem, pick_sem, t_sem, gath_send, gath_recv, back_send, back_recv, score_send, score_recv,
     small_send, small_recv, shift_send, shift_recv,
 ):
     sec = lax.axis_index("section")
     me = lax.axis_index("row")
     tokens, width = x_v.shape
+    ff = wout_v.shape[0]
     slots = n_row * CAP
     half = width // HALVES
     part = half // BANDS
@@ -41,7 +42,9 @@
 
     def win_copy(i, c):
         rows = pl.ds(c * quarter, quarter)
-        return pltpu.make_async_copy(win_hbm.at[i, rows], win_v.at[i, rows], win_sem.at[i, c])
+        return pltpu.make_async_copy(
+            win_hbm.at[i, rows], win_v.at[rows, pl.ds(i * ff, ff)], win_sem.at[i, c]
+        )
 
     wout_copy = pltpu.make_async_copy(wout_hbm, wout_v, wout_sem)
     def token_copy(k):
@@ -49,6 +52,14 @@
         cols = pl.ds(k % HALVES * half, half)
         return pltpu.make_async_copy(source.at[:, cols], to.at[:, cols], t_sem.at[k])
 
+    pick_copies = [
+        pltpu.make_async_copy(source, to, pick_sem.at[i])
+        for i, (source, to) in enumerate(
+            ((chosen_hbm, chosen_ref), (weight_hbm, weight_ref))
+        )
+    ]
+    for copy in pick_copies:
+        copy.start()
     for k in range(2 * HALVES):
         token_copy(k).start()
 
@@ -73,6 +84,9 @@
         @pl.loop(0, n_row)
         def _(r):
             pl.semaphore_signal(barrier, inc=1, device_id={"section": sec + 1, "row": r}, device_id_type=MESH)
+
+    for copy in pick_copies:
+        copy.wait()
 
     hit = (chosen_ref[...] == hot_ref[0]).astype(F32)
     hit_tok = jnp.sum(hit, axis=0, keepdims=True)
@@ -170,17 +184,16 @@
             at = h * half + c * part
             rows_ref[:, at : at + part] = rows[c * slots : (c + 1) * slots]
 
-    gate = up = None
-    for c in range(QUARTERS):
-        cols = slice(c * quarter, (c + 1) * quarter)
-        if c % (QUARTERS // HALVES) == 0:
-            gathered(c // (QUARTERS // HALVES), xs, c // (QUARTERS // HALVES))
-        win_copy(0, c).wait()
-        win_copy(1, c).wait()
-        g_part = jnp.dot(xs[:, cols], win_v[0, cols, :], preferred_element_type=F32)
-        u_part = jnp.dot(xs[:, cols], win_v[1, cols, :], preferred_element_type=F32)
-        gate = g_part if gate is None else gate + g_part
-        up = u_part if up is None else up + u_part
+    both = jnp.zeros((slots, 2 * ff), F32)
+    per = QUARTERS // HALVES
+    for h in range(HALVES):
+        gathered(h, xs, h)
+        for c in range(h * per, (h + 1) * per):
+            win_copy(0, c).wait()
+            win_copy(1, c).wait()
+        cols = slice(h * half, (h + 1) * half)
+        both = both + jnp.dot(xs[:, cols], win_v[cols, :], preferred_element_type=F32)
+    gate, up = both[:, :ff], both[:, ff:]
 
     gathered(2, gs, 0)
     gathered(3, gs, 1)
@@ -233,10 +246,17 @@
         inner = lax.rem(out_row, ROWS)
         source = (inner // CAP) * slots + (out_row // ROWS) * CAP + lax.rem(inner, CAP)
         perm = (iota((n_row * ROWS, BANDS * slots), 1) == source).astype(BF16)
+        sides_d = jnp.concatenate([dgate, dup], axis=1)
+
+        def product(q):
+            rows = slice(q * quarter, (q + 1) * quarter)
+            return lax.dot_general(win_v[rows, :], sides_d, LAST, preferred_element_type=F32)
+
+        later = product(0)
         for q in range(QUARTERS):
-            rows = slice(q * quarter, (q + 1) * quarter)
-            total = lax.dot_general(win_v[0, rows, :], dgate, LAST, preferred_element_type=F32)
-            total = total + lax.dot_general(win_v[1, rows, :], dup, LAST, preferred_element_type=F32)
+            total = later
+            if q + 1 < QUARTERS:
+                later = product(q + 1)
             back = total.T.astype(BF16)
             stack = jnp.concatenate([back[:, b * band : (b + 1) * band] for b in range(BANDS)], axis=0)
             packed = jnp.dot(perm, stack, preferred_element_type=F32).astype(BF16)
@@ -311,12 +331,14 @@
             pltpu.VMEM((tokens, width), BF16),
             pltpu.VMEM((top, tokens), F32),
         ),
-        in_specs=[pl.BlockSpec(memory_space=pltpu.SMEM), vmem, vmem, hbm, hbm, hbm, hbm],
+        in_specs=[pl.BlockSpec(memory_space=pltpu.SMEM)] + [hbm] * 6,
         out_specs=(vmem, vmem),
         scratch_shapes=[
+            pltpu.VMEM((top, tokens), jnp.int32),
+            pltpu.VMEM((top, tokens), F32),
             pltpu.VMEM((tokens, width), BF16),
             pltpu.VMEM((tokens, width), BF16),
-            pltpu.VMEM((2, width, ff), BF16),
+            pltpu.VMEM((width, 2 * ff), BF16),
             pltpu.VMEM((ff, width), BF16),
             pltpu.VMEM((2 * HALVES, n_row, ROWS, part), BF16),
             pltpu.VMEM((slots, width), BF16),
@@ -329,6 +351,7 @@
             pltpu.VMEM((n_row, 8, 128), F32),
             dma((2, QUARTERS)),
             dma,
+            dma((2,)),
             dma((2 * HALVES,)),
             dma((2 * HALVES,)),
             dma((2 * HALVES,)),

time: 30 us -> 31 us (1.033)
  Pallas kernels: 27 us -> 28 us
    pallas_call x1, Pallas kernels: 27 us -> 28 us  [on_device(): pl.pallas_call(functools.partial(expert_kernel, n_row, n_sec), out_shape=...]
where the time goes in v6:
time: 31 us; the launch traced here: 30.9 us
  Pallas kernels  28 us (90%)
  local copies, waits for them, and re-layouts  1.53 us (5%)
  between operations  1.29 us (4%)
    pallas_call x1, Pallas kernels, on_device(): pl.pallas_call(functools.partial(expert_kernel, n_row, n_sec), out_shape=...  28 us
    unnamed x2, local copies, waits for them, and re-layouts  1.53 us

profile of v6, /device:TPU:1, one launch (start us, length us, event | category | flops | bytes accessed | tf_op | source)
XLA Modules:
  0.0 30.9 jit_solution(2527839900744753250)
XLA Ops:
  1.3 28.0 %expert.1 = (bf16[128,4096]{1,0:T(8,128)(2,1)S(1)}, f32[2,128]{1,0:T(2,128)S(1)}) custom-call(s32[1]{0:T(128)S(6)} %copy.13.hot_ref, s32[2,128]{1,0:T(2,128)} %bitcast.20, f32[2,128]{1,0:T(2,128)} %bitcast.21, bf16[128,4096]{1,0:T(8,128)(2,1)} %bitcast.18, bf16[128,4096]{1,0:T(8,128)(2,1)} %bitcast.19, bf16[2,4096,896]{2,1,0:T(8,128)(2,1)} %bitcast.16, ...), custom_call_target="tpu_custom_call" | custom-call | flops 587202560 | bytes 22020096 | tf_op jit(solution)/shard_map/expert/pallas_call | solution.py:328
  29.3 1.0 %copy.11 = bf16[1,128,4096]{2,1,0:T(8,128)(2,1)} copy(bf16[1,128,4096]{2,1,0:T(8,128)(2,1)S(1)} %bitcast.14) | data formatting | bytes 2097152
  30.3 0.6 %copy.12 = f32[1,128,2]{1,2,0:T(2,128)} copy(f32[1,128,2]{1,2,0:T(2,128)S(1)} %bitcast.15) | data formatting | bytes 2048

commit v7 on v5

--- a/solution.py
+++ b/solution.py
@@ -23,11 +23,11 @@
 
 
 def expert_kernel(
-    n_row, n_sec, hot_ref, chosen_ref, weight_ref, x_hbm, cot_hbm, win_hbm, wout_hbm,
+    n_row, n_sec, hot_ref, chosen_hbm, weight_hbm, x_hbm, cot_hbm, win_hbm, wout_hbm,
     moved_out, grad_out,
-    x_v, cot_v, win_v, wout_v, gath, xs, gs, pack, land,
+    chosen_ref, weight_ref, x_v, cot_v, win_v, wout_v, gath, xs, gs, pack, land,
     scale_v, scale_land, score_v, score_land,
-    win_sem, wout_sem, t_sem, gath_send, gath_recv, back_send, back_recv, score_send, score_recv,
+    win_sem, wout_sem, pick_sem, t_sem, gath_send, gath_recv, back_send, back_recv, score_send, score_recv,
     small_send, small_recv, shift_send, shift_recv,
 ):
     sec = lax.axis_index("section")
@@ -49,6 +49,12 @@
         cols = pl.ds(k % HALVES * half, half)
         return pltpu.make_async_copy(source.at[:, cols], to.at[:, cols], t_sem.at[k])
 
+    pick_copies = [
+        pltpu.make_async_copy(source, to, pick_sem.at[i])
+        for i, (source, to) in enumerate(((chosen_hbm, chosen_ref), (weight_hbm, weight_ref)))
+    ]
+    for copy in pick_copies:
+        copy.start()
     for k in range(2 * HALVES):
         token_copy(k).start()
 
@@ -73,6 +79,9 @@
         @pl.loop(0, n_row)
         def _(r):
             pl.semaphore_signal(barrier, inc=1, device_id={"section": sec + 1, "row": r}, device_id_type=MESH)
+
+    for copy in pick_copies:
+        copy.wait()
 
     hit = (chosen_ref[...] == hot_ref[0]).astype(F32)
     hit_tok = jnp.sum(hit, axis=0, keepdims=True)
@@ -131,21 +140,19 @@
         scale_v, scale_land, small_send, small_recv, device_id=prev, device_id_type=MESH
     )
 
-    token_copy(0).wait()
-    held_rows(0)
-    sides = has_prev.astype(jnp.int32) + has_next.astype(jnp.int32)
-    pl.semaphore_wait(barrier, n_row - 1 + n_row * sides)
-    send_rows(0)
-    token_copy(1).wait()
-    held_rows(1)
-    send_rows(1)
-
-    for k in range(HALVES, 2 * HALVES):
+    for k in range(2 * HALVES):
         token_copy(k).wait()
+        if k < HALVES:
+            held_rows(k)
     for c in range(QUARTERS):
         win_copy(0, c).start()
         win_copy(1, c).start()
     wout_copy.start()
+
+    sides = has_prev.astype(jnp.int32) + has_next.astype(jnp.int32)
+    pl.semaphore_wait(barrier, n_row - 1 + n_row * sides)
+    for k in range(HALVES):
+        send_rows(k)
 
     for k in range(HALVES, 2 * HALVES):
         held_rows(k)
@@ -311,9 +318,11 @@
             pltpu.VMEM((tokens, width), BF16),
             pltpu.VMEM((top, tokens), F32),
         ),
-        in_specs=[pl.BlockSpec(memory_space=pltpu.SMEM), vmem, vmem, hbm, hbm, hbm, hbm],
+        in_specs=[pl.BlockSpec(memory_space=pltpu.SMEM)] + [hbm] * 6,
         out_specs=(vmem, vmem),
         scratch_shapes=[
+            pltpu.VMEM((top, tokens), jnp.int32),
+            pltpu.VMEM((top, tokens), F32),
             pltpu.VMEM((tokens, width), BF16),
             pltpu.VMEM((tokens, width), BF16),
             pltpu.VMEM((2, width, ff), BF16),
@@ -329,6 +338,7 @@
             pltpu.VMEM((n_row, 8, 128), F32),
             dma((2, QUARTERS)),
             dma,
+            dma((2,)),
             dma((2 * HALVES,)),
             dma((2 * HALVES,)),
             dma((2 * HALVES,)),

time: 30 us -> 29.5 us (0.983)
  Pallas kernels: 27 us -> 26.5 us
    pallas_call x1, Pallas kernels: 27 us -> 26.5 us  [on_device(): pl.pallas_call(functools.partial(expert_kernel, n_row, n_sec), out_shape=...]
where the time goes in v7:
time: 29.5 us; the launch traced here: 29.3 us
  Pallas kernels  26.5 us (90%)
  local copies, waits for them, and re-layouts  1.53 us (5%)
  between operations  1.29 us (4%)
    pallas_call x1, Pallas kernels, on_device(): pl.pallas_call(functools.partial(expert_kernel, n_row, n_sec), out_shape=...  26.5 us
    unnamed x2, local copies, waits for them, and re-layouts  1.53 us

profile of v7, /device:TPU:1, one launch (start us, length us, event | category | flops | bytes accessed | tf_op | source)
XLA Modules:
  0.0 29.3 jit_solution(148352028737096345)
XLA Ops:
  1.3 26.5 %expert.1 = (bf16[128,4096]{1,0:T(8,128)(2,1)S(1)}, f32[2,128]{1,0:T(2,128)S(1)}) custom-call(s32[1]{0:T(128)S(6)} %copy.13.hot_ref, s32[2,128]{1,0:T(2,128)} %bitcast.20, f32[2,128]{1,0:T(2,128)} %bitcast.21, bf16[128,4096]{1,0:T(8,128)(2,1)} %bitcast.18, bf16[128,4096]{1,0:T(8,128)(2,1)} %bitcast.19, bf16[2,4096,896]{2,1,0:T(8,128)(2,1)} %bitcast.16, ...), custom_call_target="tpu_custom_call" | custom-call | flops 587202560 | bytes 22020096 | tf_op jit(solution)/shard_map/expert/pallas_call | solution.py:315
  27.8 1.0 %copy.11 = bf16[1,128,4096]{2,1,0:T(8,128)(2,1)} copy(bf16[1,128,4096]{2,1,0:T(8,128)(2,1)S(1)} %bitcast.14) | data formatting | bytes 2097152
  28.7 0.6 %copy.12 = f32[1,128,2]{1,2,0:T(2,128)} copy(f32[1,128,2]{1,2,0:T(2,128)S(1)} %bitcast.15) | data formatting | bytes 2048
